TPU v7x, 512 devices: a whole 4x8x8 slice. The times are simulated.
512 devices in a mesh: chan: 32 (over y, z_hi, core), stn: 16 (over x, z_lo).
Axes of the slice: x: 4, y: 8, z: 8 (z_hi: 2, z_lo: 4; z = z_hi * 4 + z_lo), core: 2. Of those that a mesh axis runs over, the one named last changes fastest.
Arguments:
- voltages: bfloat16 [16, 32, 2, 253952], P('stn', 'chan'), may hold values from -6 to 6
- station_gains: bfloat16 [512, 16, 128], P('chan', 'stn'), may hold values from -3.6 to 3.6
- positions: float32 [512, 2], replicated, may hold values from -64 to 64
- directions: float32 [32, 2], replicated, may hold values from -0.5 to 0.5
- weights: float32 [32, 2], replicated, may hold values from 0.03 to 0.15
- baseline_flags: int32 [512, 512], P('stn'), may hold values from 0 to 1, as said below
Outputs:
- gain_steps: float32 [512, 16, 128], P('chan', 'stn')
Inputs may be any that keep to these rules, and one draw needn't show every extreme that they name: symmetric: baseline_flags[s, r] equals baseline_flags[r, s].
All inputs are finite; a program needn't handle non-finite values.
Results may differ from a plain program's by a relative error of at most 0.00099.
Values may be sent and summed in bfloat16 or wider, within the bound.
No kernel may reach another device: no remote copies, remote signals or barrier semaphores. Data moves between devices by JAX's collectives and lax.ppermute only.
A program may use at most 128 MiB of HBM per device.

v0:
```python
import math

import jax
import jax.numpy as jnp
from jax import lax
from jax.sharding import PartitionSpec as P

F = 4096
FRAME = 8192
TAPS = 16


def filter_table(tap_count, frame_len):
    total_len = tap_count * frame_len
    sample_ids = jnp.arange(total_len, dtype=jnp.float32)
    offset = (sample_ids + 0.5 - total_len / 2) / frame_len
    window = (
        jnp.sin(jnp.pi * offset)
        / (jnp.pi * offset)
        * (0.5 - 0.5 * jnp.cos(2 * jnp.pi * sample_ids / total_len))
    )
    return window.reshape(tap_count, frame_len)


def steering(pos_rows, directions, weights, channels):
    delays = (
        pos_rows[:, 0][:, None] * directions[:, 0][None, :]
        + pos_rows[:, 1][:, None] * directions[:, 1][None, :]
    )
    scaled = 2.0 * math.pi * (1.0 + channels.astype(jnp.float32) / F)
    phases = scaled[:, None, None] * delays[None]
    real_part = jnp.cos(phases)[..., None] * weights[None, None]
    imag_part = -jnp.sin(phases)[..., None] * weights[None, None]
    stacked = jnp.transpose(jnp.stack([real_part, imag_part], axis=1), (0, 3, 1, 2, 4))
    return stacked.reshape(channels.shape[0], directions.shape[0], -1).astype(jnp.bfloat16)


def cosine_table(row_count, col_count, period):
    angles = (
        jnp.arange(row_count, dtype=jnp.int32)[:, None]
        * jnp.arange(col_count, dtype=jnp.int32)[None, :]
        % period
    )
    angles = angles.astype(jnp.float32) * (2.0 * math.pi / period)
    return (jnp.cos(angles), jnp.sin(angles))


def filterbank(samples, frames, kept_chans):
    tap_count = samples.shape[1] - frames + 1
    frame_len = samples.shape[2]
    streams = samples.shape[0]
    window = filter_table(tap_count, frame_len)
    filtered = jnp.zeros((streams, frames, frame_len), jnp.float32)
    for tap_index in range(tap_count):
        filtered = (
            filtered
            + samples[:, tap_index : tap_index + frames, :].astype(jnp.float32) * window[tap_index]
        )
    outer_len = frame_len // 128
    shaped = filtered.reshape(streams, frames, outer_len, 128)
    first_cos, first_sin = cosine_table(outer_len, outer_len, outer_len)
    middle = lax.Precision.HIGH
    section_re = jnp.einsum("kj,stjm->stkm", first_cos, shaped, precision=middle)
    section_im = -jnp.einsum("kj,stjm->stkm", first_sin, shaped, precision=middle)
    twist_cos, twist_sin = cosine_table(outer_len, 128, frame_len)
    turned_re = section_re * twist_cos + section_im * twist_sin
    turned_im = section_im * twist_cos - section_re * twist_sin
    second_cos, second_sin = cosine_table(kept_chans // outer_len, 128, 128)
    out_re = jnp.einsum("bn,stan->bats", second_cos, turned_re, precision=middle) + jnp.einsum(
        "bn,stan->bats", second_sin, turned_im, precision=middle
    )
    out_im = jnp.einsum("bn,stan->bats", second_cos, turned_im, precision=middle) - jnp.einsum(
        "bn,stan->bats", second_sin, turned_re, precision=middle
    )
    spectra = jnp.stack([out_re, out_im], axis=3).reshape(kept_chans, frames, 2, streams)
    return (spectra / math.sqrt(frame_len)).astype(jnp.bfloat16)


def complex_products(near_side, far_side, divisor):
    chans = near_side.shape[0]
    length = near_side.shape[1]
    half_width = near_side.shape[2] // 2
    near_split = near_side.reshape(chans, length, 2, half_width)
    real_far = far_side[:, :, 0]
    imag_far = far_side[:, :, 1]
    paired = jnp.stack(
        [jnp.stack([real_far, -imag_far], axis=3), jnp.stack([imag_far, real_far], axis=3)], axis=2
    )
    paired = paired.reshape(chans, length, 2, far_side.shape[3], 2 * half_width)
    product = jnp.einsum("clru,clrnw->cnuw", near_split, paired, preferred_element_type=jnp.float32)
    return (product[..., :half_width] / divisor, product[..., half_width:] / divisor)


def residual_terms(vis_re, vis_im, mod_re, mod_im, near_gain, far_gain, usable):
    half_width = vis_re.shape[-1]
    exact = lax.Precision.HIGHEST
    near_re = near_gain[:, :half_width]
    near_im = near_gain[:, half_width:]
    far_re = far_gain[:, :, :half_width]
    far_im = far_gain[:, :, half_width:]
    cross_re = usable * (vis_re * mod_re + vis_im * mod_im)
    cross_im = usable * (vis_im * mod_re - vis_re * mod_im)
    power = usable * (mod_re * mod_re + mod_im * mod_im)
    far_power = far_re * far_re + far_im * far_im
    sum_re = jnp.einsum("cnuw,cnw->cu", cross_re, far_re, precision=exact) - jnp.einsum(
        "cnuw,cnw->cu", cross_im, far_im, precision=exact
    )
    sum_im = jnp.einsum("cnuw,cnw->cu", cross_re, far_im, precision=exact) + jnp.einsum(
        "cnuw,cnw->cu", cross_im, far_re, precision=exact
    )
    weight_sum = jnp.einsum("cnuw,cnw->cu", power, far_power, precision=exact)
    num_re = sum_re - near_re * weight_sum
    num_im = sum_im - near_im * weight_sum
    own_terms = (jnp.concatenate([num_re, num_im], axis=1), weight_sum)
    return own_terms


def build_mask(flag_rows, row_first, piece_count, block_stations, pol_count):
    row_ids = row_first + jnp.arange(block_stations, dtype=jnp.int32)[:, None]
    col_ids = jnp.arange(piece_count * block_stations, dtype=jnp.int32)[None, :]
    allowed = jnp.where(row_ids != col_ids, flag_rows, 0).astype(jnp.float32)
    allowed = jnp.transpose(allowed.reshape(block_stations, piece_count, block_stations), (1, 0, 2))
    allowed = jnp.broadcast_to(
        allowed[:, :, None, :, None],
        (piece_count, block_stations, pol_count, block_stations, pol_count),
    )
    return allowed.reshape(piece_count, block_stations * pol_count, block_stations * pol_count)


def sweep(
    near_block,
    near_steer,
    near_gain,
    far_block,
    far_gain,
    far_pos,
    usable,
    channels,
    directions,
    weights,
):
    chans_dev = near_block.shape[0]
    frames = near_block.shape[1]
    pieces = far_block.shape[2]
    streams = near_block.shape[2] // 2
    sources = directions.shape[0]
    group_size = 1
    while chans_dev % (2 * group_size) == 0 and 2 * group_size * pieces <= 64:
        group_size = group_size * 2
    rounds = chans_dev // group_size

    def regroup(values):
        return values.reshape((rounds, group_size) + values.shape[1:])

    def one_round(state_in, inputs):
        x_near, e_near, g_near, x_far, g_far, chan_ids = inputs
        x_far = jnp.transpose(
            x_far.reshape(group_size, frames, pieces, 2, streams), (0, 1, 3, 2, 4)
        )
        e_far = steering(far_pos, directions, weights, chan_ids).reshape(
            group_size, sources, 2, pieces, streams
        )
        vis_re, vis_im = complex_products(x_near, x_far, frames)
        mod_re, mod_im = complex_products(e_near, e_far, 1)
        return (state_in, residual_terms(vis_re, vis_im, mod_re, mod_im, g_near, g_far, usable))

    inputs = (
        regroup(near_block),
        regroup(near_steer),
        regroup(near_gain),
        regroup(far_block),
        regroup(far_gain),
        regroup(channels),
    )
    unused, results = lax.scan(one_round, 0, inputs)
    return tuple(
        (result_part.reshape((chans_dev,) + result_part.shape[2:]) for result_part in results)
    )


def body(voltages, station_gains, positions, directions, weights, baseline_flags):
    chan_count = lax.axis_size("chan")
    chan_index = lax.axis_index("chan")
    stn_index = lax.axis_index("stn")
    local_stations = voltages.shape[1]
    pol_count = voltages.shape[2]
    frames = voltages.shape[3] // FRAME - TAPS + 1
    samples = voltages.reshape(local_stations * pol_count, frames + TAPS - 1, FRAME)
    chans_dev = station_gains.shape[0]
    spectra = filterbank(samples, frames, chans_dev * chan_count)
    packed = spectra.reshape(chan_count, -1)
    arrived = lax.all_to_all(packed, "chan", split_axis=0, concat_axis=0, tiled=True)
    arrived = arrived.reshape(chan_count, chans_dev, frames, 2, local_stations * pol_count)
    own_block = jnp.transpose(arrived, (1, 2, 3, 0, 4)).reshape(chans_dev, frames, -1)
    streams = own_block.shape[2] // 2
    block_stations = streams // pol_count
    channels = chan_index * chans_dev + jnp.arange(chans_dev, dtype=jnp.int32)
    first_station = stn_index * block_stations
    own_pos = lax.dynamic_slice_in_dim(positions, first_station, block_stations, 0)
    own_steer = steering(own_pos, directions, weights, channels)
    own_gain = station_gains[:, 0, :].astype(jnp.float32)
    far_seed = own_block[:, :, None, :]
    gain_seed = station_gains[:, None]
    far_block = lax.all_gather(far_seed, "stn", axis=2, tiled=True)
    far_gain = lax.all_gather(gain_seed, "stn", axis=2, tiled=True)[:, 0].astype(jnp.float32)
    piece_count = far_block.shape[2]
    usable = build_mask(baseline_flags, first_station, piece_count, block_stations, pol_count)
    own_num, own_den = sweep(
        own_block,
        own_steer,
        own_gain,
        far_block,
        far_gain,
        positions,
        usable,
        channels,
        directions,
        weights,
    )
    denominator = 1.0 + own_den
    steps_out = own_num / jnp.concatenate([denominator, denominator], axis=1)
    return steps_out[:, None, :]


def solution(mesh):
    in_specs = (P("stn", "chan", None, None), P("chan", "stn", None), P(), P(), P(), P("stn", None))
    out_specs = P("chan", "stn", None)
    return jax.shard_map(body, mesh=mesh, in_specs=in_specs, out_specs=out_specs, check_vma=False)
```

profile of v0, /device:TPU:8, one launch (start us, length us, event | category | flops | bytes accessed | tf_op | source)
XLA Modules:
  0.0 311.5 jit_solution(7750985458911342803)
XLA Ops:
  6.5 3.6 %fusion.31 = f32[131072]{0:T(1024)S(1)} fusion(), kind=kLoop, calls=%fused_computation.75 | loop fusion | flops 917504 | bytes 524288 | tf_op jit(solution)/shard_map/mul | solution.py:18
  10.9 2.3 multiply_add_fusion.3
  20.5 5.5 %copy.40 = bf16[512,16,2,2]{3,2,1,0:T(2,128)(2,1)} copy(bf16[512,16,2,2]{0,1,3,2:T(8,128)(2,1)S(1)} %fusion.38) | data formatting | bytes 131072 | tf_op jit(solution)/shard_map/convert_element_type | solution.py:76
  26.0 7.2 %convert_element_type.175 = bf16[32,1,1024]{2,1,0:T(2,128)(2,1)S(1)} reshape(bf16[512,16,2,2]{3,2,1,0:T(2,128)(2,1)} %copy.40) | data formatting | bytes 131072 | tf_op jit(solution)/shard_map/convert_element_type | solution.py:76
  34.8 27.6 %all_to_all.6 = bf16[32,2,512]{2,1,0:T(2,128)(2,1)S(1)} all-to-all(bf16[32,2,512]{2,1,0:T(2,128)(2,1)S(1)} %reshape.440), channel_id=1, replica_groups=mesh['chan'=32,'stn'=16] {'chan'}, dimensions={0} | all-to-all | bytes 131072 | tf_op jit(solution)/shard_map/all_to_all | solution.py:192
  69.3 42.7 %all-gather = bf16[16,16,128]{2,0,1:T(8,128)(2,1)S(1)} all-gather(bf16[16,1,128]{2,0,1:T(8,128)(2,1)S(1)} %copy-done.5), channel_id=2, replica_groups=mesh['chan'=32,'stn'=16] {'stn'}, dimensions={1}, use_global_device_ids=true | all-gather | bytes 69632 | tf_op jit(solution)/shard_map/all_gather | solution.py:205
  114.4 30.7 %all-gather.3.cloned.1.call-done = bf16[16,16,16,128]{3,1,0,2:T(8,128)(2,1)} async-done(((bf16[16,16,1,128]{3,1,0,2:T(8,128)(2,1)}), bf16[16,16,16,128]{3,1,0,2:T(8,128)(2,1)}) %all-gather.3.cloned.1.call-update) | async-done | bytes 1048592 | tf_op jit(solution)/shard_map/all_gather | solution.py:204
  145.1 157.0 %while.13 = (s32[]{:T(128)}, f32[4,4,128]{2,1,0:T(4,128)}, f32[4,4,64]{2,1,0:T(4,128)}, bf16[4,4,16,16,128]{4,2,1,0,3:T(8,128)(2,1)}, bf16[4,4,16,128]{3,2,1,0:T...) while((s32[]{:T(128)}, f32[4,4,128]{2,1,0:T(4,128)}, ...), condition=%wide.region_1.2_spmd.clone, body=%wide.region_0.1_spmd.clone.sunk | while | flops 122812432 | bytes 41164008 | solution.py:175
  164.2 2.3 broadcast_in_dim.31
  166.5 2.3 copy.107
  168.8 3.4 %subtract_multiply_fusion.2 = (f32[4,16,64,64]{3,2,1,0:T(8,128)S(1)}, f32[4,16,64,64]{3,2,1,0:T(8,128)S(1)}) fusion(f32[4,16,64,128]{3,2,1,0:T(8,128)} %convolution_bitcast_fusion.6, f32[4,16,64,128]{3,2,1,0:T(8,128)S(1)} %convolution_bitcast_fusion.5, f32[16,64,64]{2,1,0:T(8,128)S(1)} %copy.107), kind=kLoop, calls=%fused_computation.8.clone.1 | loop fusion | flops 2621440 | bytes 6553600 | tf_op jit(solution)/shard_map/while/body/eval_jaxpr/mul | solution.py:102
  180.9 2.3 fusion.160
  203.4 2.3 broadcast_in_dim.31
  205.7 2.3 copy.107
  208.0 3.4 %subtract_multiply_fusion.2 = (f32[4,16,64,64]{3,2,1,0:T(8,128)S(1)}, f32[4,16,64,64]{3,2,1,0:T(8,128)S(1)}) fusion(f32[4,16,64,128]{3,2,1,0:T(8,128)} %convolution_bitcast_fusion.6, f32[4,16,64,128]{3,2,1,0:T(8,128)S(1)} %convolution_bitcast_fusion.5, f32[16,64,64]{2,1,0:T(8,128)S(1)} %copy.107), kind=kLoop, calls=%fused_computation.8.clone.1 | loop fusion | flops 2621440 | bytes 6553600 | tf_op jit(solution)/shard_map/while/body/eval_jaxpr/mul | solution.py:102
  220.1 2.3 fusion.160
  242.6 2.3 broadcast_in_dim.31
  244.9 2.3 copy.107
  247.2 3.4 %subtract_multiply_fusion.2 = (f32[4,16,64,64]{3,2,1,0:T(8,128)S(1)}, f32[4,16,64,64]{3,2,1,0:T(8,128)S(1)}) fusion(f32[4,16,64,128]{3,2,1,0:T(8,128)} %convolution_bitcast_fusion.6, f32[4,16,64,128]{3,2,1,0:T(8,128)S(1)} %convolution_bitcast_fusion.5, f32[16,64,64]{2,1,0:T(8,128)S(1)} %copy.107), kind=kLoop, calls=%fused_computation.8.clone.1 | loop fusion | flops 2621440 | bytes 6553600 | tf_op jit(solution)/shard_map/while/body/eval_jaxpr/mul | solution.py:102
  259.3 2.3 fusion.160
  281.8 2.3 broadcast_in_dim.31
  284.1 2.3 copy.107
  286.4 3.4 %subtract_multiply_fusion.2 = (f32[4,16,64,64]{3,2,1,0:T(8,128)S(1)}, f32[4,16,64,64]{3,2,1,0:T(8,128)S(1)}) fusion(f32[4,16,64,128]{3,2,1,0:T(8,128)} %convolution_bitcast_fusion.6, f32[4,16,64,128]{3,2,1,0:T(8,128)S(1)} %convolution_bitcast_fusion.5, f32[16,64,64]{2,1,0:T(8,128)S(1)} %copy.107), kind=kLoop, calls=%fused_computation.8.clone.1 | loop fusion | flops 2621440 | bytes 6553600 | tf_op jit(solution)/shard_map/while/body/eval_jaxpr/mul | solution.py:102
  298.5 2.3 fusion.160
  (241 shorter events, 135.5 us)
Async XLA Ops:
  6.5 3.8 %copy-start.1 = (bf16[1,1,2,253952]{3,2,1,0:T(2,128)(2,1)S(1)}, bf16[1,1,2,253952]{3,2,1,0:T(2,128)(2,1)}, u32[]{:S(2)}) copy-start(bf16[1,1,2,253952]{3,2,1,0:T(2,128)(2,1)} %param.8) | copy-start | bytes 3047428
  6.5 138.6 %all-gather.3.cloned.1.call-start = ((), (), s32[]{:S(2)}) async-start(), calls=%async_computation.1 | async-start | bytes 1114112 | tf_op jit(solution)/shard_map/all_gather | solution.py:204
  33.2 31.4 %copy-start.2 = (f32[512,2]{0,1:T(2,128)S(1)}, f32[512,2]{0,1:T(2,128)}, u32[]{:S(2)}) copy-start(f32[512,2]{0,1:T(2,128)} %param.10) | copy-start | bytes 12292
  33.2 33.3 %copy-start.4 = (f32[32,2]{0,1:T(2,128)S(1)}, f32[32,2]{0,1:T(2,128)}, u32[]{:S(2)}) copy-start(f32[32,2]{0,1:T(2,128)} %param.12) | copy-start | bytes 772
  63.5 4.6 %copy-start.3 = (s32[32,512]{1,0:T(8,128)S(1)}, s32[32,512]{1,0:T(8,128)}, u32[]{:S(2)}) copy-start(s32[32,512]{1,0:T(8,128)} %param.13) | copy-start | bytes 196612
  66.5 2.8 copy-start.5
  161.4 2.7 copy-start
  200.7 2.7 copy-start
  239.9 2.7 copy-start
  279.1 2.7 copy-start
Sparse Core Ops, SparseCore 0:
  64.7 80.4 all-gather.2
where the time goes:
time: 317 us; the launch traced here: 311 us
  local copies, waits for them, and re-layouts  98 us (31%)
  blocking collectives  70.2 us (22%)
  matrix products  56.6 us (18%)
  other arithmetic  40.8 us (13%)
  waiting for transfers between devices  30.7 us (10%)
  between operations  14 us (4%)
    all_gather x1, blocking collectives, body(): lax.all_gather(gain_seed, 'stn', axis=2, tiled=True)[:, 0]  42.7 us
    all_gather x1, waiting for transfers between devices, body(): far_block = lax.all_gather(far_seed, 'stn', axis=2, tiled=True)  30.7 us
    all_to_all x1, blocking collectives, body(): lax.all_to_all(packed, 'chan', split_axis=0, concat_axis=0, tiled=True)  27.6 us
    slice x12, local copies, waits for them, and re-layouts, complex_products(): imag_far = far_side[:, :, 1]  14.7 us
    mul x4, other arithmetic, residual_terms(): cross_im = usable * (vis_im * mod_re - vis_re * mod_im)  13.5 us
    convert_element_type x3, local copies, waits for them, and re-layouts, filterbank(): return (spectra / math.sqrt(frame_len)).astype(jnp.bfloat16)  13.2 us
    dynamic_slice x24, local copies, waits for them, and re-layouts, sweep(): unused, results = lax.scan(one_round, 0, inputs)  10.9 us
    broadcast_in_dim x4, local copies, waits for them, and re-layouts, build_mask(): jnp.broadcast_to(allowed[:, :, None, :, None], (piece_count, block_statio...  9.34 us
  transfers between devices with their start and end apart: 1, of which 1 were waited for; matrix products, arithmetic and copies ran while one was open for 2% of the time, Pallas kernels for 0%

commit v1 on v0

v1 whole, which is shorter than its diff:
```python
import math

import jax
import jax.numpy as jnp
import numpy as np
from jax import lax
from jax.experimental import pallas as pl
from jax.experimental.pallas import tpu as pltpu
from jax.sharding import PartitionSpec as P

F = 4096
CW = 512
FRAME = 8192
TAPS = 16
STATIONS = 512
NFRAMES = 16
SOURCES = 32
BLOCKS = 16
SPB = 32
FRAMES_IN = NFRAMES + TAPS - 1
BF = jnp.bfloat16
F32 = jnp.float32


def split_np(values):
    hi = values.astype(jnp.bfloat16)
    lo = (values - hi.astype(np.float64)).astype(jnp.bfloat16)
    return hi, lo


def filter_tables():
    n = np.arange(TAPS * FRAME, dtype=np.float64)
    q = (n + 0.5 - TAPS * FRAME / 2) / FRAME
    window = np.sin(np.pi * q) / (np.pi * q) * (0.5 - 0.5 * np.cos(2 * np.pi * n / (TAPS * FRAME)))
    window = window.astype(np.float32).reshape(TAPS, 64, 128)
    k = np.arange(64)[:, None]
    j = np.arange(64)[None, :]
    angle = 2 * np.pi * (k * j % 64) / 64
    first = np.concatenate([np.cos(angle), -np.sin(angle)], axis=0)
    hi, lo = split_np(first)
    first = np.concatenate([hi, hi, lo], axis=1)
    m = np.arange(128)[None, :]
    angle = 2 * np.pi * (k * m % 8192) / 8192
    turn = np.stack([np.cos(angle), np.sin(angle)]).astype(np.float32)
    b = np.arange(8)[None, :]
    mm = np.arange(128)[:, None]
    angle = 2 * np.pi * (b * mm % 128) / 128
    c = np.cos(angle) / math.sqrt(FRAME)
    s = np.sin(angle) / math.sqrt(FRAME)
    to_re = np.concatenate([c, s], axis=0)
    to_im = np.concatenate([-s, c], axis=0)
    second = np.stack([to_re, to_im], axis=2)
    second = np.broadcast_to(second[..., None], (256, 8, 2, NFRAMES)).reshape(256, 256)
    hi, lo = split_np(second)
    return window, first, turn, np.stack([hi, lo])


def split2(x):
    hi = x.astype(BF)
    return hi, (x - hi.astype(F32)).astype(BF)


def dot(a, b):
    return lax.dot_general(a, b, (((1,), (0,)), ((), ())), preferred_element_type=F32)


def dot_nt(a, b):
    return lax.dot_general(a, b, (((1,), (1,)), ((), ())), preferred_element_type=F32)


def iota(shape, dim):
    return lax.broadcasted_iota(jnp.int32, shape, dim)


def spectra_kernel(
    index_ref, volt_ref, win_ref, first_ref, turn_ref, second_ref, gain_ref, flag_ref, out_ref, fold, part
):
    def chunk(step, carry):
        stream = step // 4
        row = pl.multiple_of((step % 4) * 16, 16)
        x = volt_ref[stream, :, pl.ds(row, 16), :].astype(F32)
        acc = x[0:NFRAMES] * win_ref[0, pl.ds(row, 16), :][None]
        for tap in range(1, TAPS):
            acc = acc + x[tap : tap + NFRAMES] * win_ref[tap, pl.ds(row, 16), :][None]
        hi, lo = split2(acc)
        for t in range(NFRAMES):
            fold[stream * NFRAMES + t, pl.ds(row, 16), :] = hi[t]
            fold[stream * NFRAMES + t, pl.ds(pl.multiple_of(row + 64, 16), 16), :] = lo[t]
            fold[stream * NFRAMES + t, pl.ds(pl.multiple_of(row + 128, 16), 16), :] = hi[t]
        return carry

    lax.fori_loop(0, 8, chunk, 0)

    turn_cos = turn_ref[0]
    turn_sin = turn_ref[1]
    first = first_ref[...]
    column = iota((1, 256), 1) % NFRAMES
    total = jnp.zeros((128, 256), F32)
    for t in range(NFRAMES):
        rows = []
        for stream in range(2):
            section = dot(first, fold[stream * NFRAMES + t])
            re, im = section[0:64], section[64:128]
            rows.append(
                jnp.concatenate(
                    [re * turn_cos + im * turn_sin, im * turn_cos - re * turn_sin], axis=1
                )
            )
        hi, lo = split2(jnp.concatenate(rows, axis=0))
        here = jnp.where(column == t, 1.0, 0.0).astype(BF)
        table_hi = second_ref[0] * here
        table_lo = second_ref[1] * here
        total = total + (dot(hi, table_hi) + dot(lo, table_hi) + dot(hi, table_lo))

    index = index_ref[0]
    flags = jnp.broadcast_to(flag_ref[pl.ds(index, 1), :].astype(F32), (8, STATIONS)).astype(BF)
    place = (iota((STATIONS, 384), 1) + 64 * (index // 4)) & (STATIONS - 1)
    wanted = (place & 15) * SPB + lax.shift_right_logical(place, 4)
    pick = jnp.where(iota((STATIONS, 384), 0) == wanted, 1.0, 0.0).astype(BF)
    row = dot(flags, pick)[0:1]

    for b in range(8):
        lanes = [
            total[0:64, b * 32 : b * 32 + 32],
            total[64:128, b * 32 : b * 32 + 32],
            jnp.broadcast_to(row[:, 0:64], (64, 64)),
        ]
        part[pl.ds(b * 256, 64, stride=4), :] = jnp.concatenate(lanes, axis=1)
    part[pl.ds(1, 512, stride=4), :] = jnp.broadcast_to(row[:, 64:192], (512, 128))
    part[pl.ds(2, 512, stride=4), :] = jnp.broadcast_to(row[:, 192:320], (512, 128))
    gains = gain_ref[...].astype(F32)
    for i in range(32):
        part[pl.ds(i * 64 + 3, 16, stride=4), :] = gains
    out_ref[...] = part[...].astype(BF)


def pair_kernel(
    index_ref, recv_ref, cos_ref, sin_ref, weight_ref, out_ref, part, near_x, near_e, far_e, usable, acc
):
    part[...] = recv_ref[...].astype(F32)
    first = part[pl.ds(0, 512, stride=4), :]
    index = index_ref[0]

    sent = jnp.concatenate(
        [
            first[:, 64:128],
            part[pl.ds(1, 512, stride=4), :],
            part[pl.ds(2, 512, stride=4), :],
        ],
        axis=1,
    )
    empty = jnp.zeros((64, 64), F32)
    for a in range(8):
        pieces = []
        for b in range(8):
            d = (b - a) % 8
            pieces.append(sent[a * 64 : a * 64 + 64, d * 64 : d * 64 + 64] if d <= 4 else empty)
        usable[pl.ds(a * 64, 64), :] = jnp.concatenate(pieces, axis=1)
    brought = usable[...]
    rows, cols = iota((512, 512), 0), iota((512, 512), 1)
    ahead = (lax.shift_right_logical(cols, 6) - lax.shift_right_logical(rows, 6)) & 7
    both = jnp.where(ahead <= 4, brought, brought.T)
    usable[...] = jnp.where(rows == cols, 0.0, both)

    xt = first.T
    zero32 = jnp.zeros((32, 512), F32)
    for p in range(2):
        own = xt[p * 32 : p * 32 + 32]
        other = jnp.concatenate([own[16:32], -own[0:16]], axis=0)
        for c, block in enumerate((own, other)):
            for q in range(2):
                whole = [zero32, zero32, zero32, zero32]
                whole[q] = block
                near_x[p, c, q] = jnp.concatenate(whole, axis=0).astype(BF)

    cos, sin = cos_ref[...], sin_ref[...]
    zero64 = jnp.zeros((64, 512), F32)
    steer, turned = [], []
    for p in range(2):
        weight = weight_ref[:, p : p + 1]
        re = (cos * weight).astype(BF).astype(F32)
        im = (-sin * weight).astype(BF).astype(F32)
        steer += [re, im]
        turned += [-im, re]
        for c, block in enumerate(((re, im), (-im, re))):
            for q in range(2):
                half = [zero64, zero64]
                half[q] = jnp.concatenate(block, axis=0)
                near_e[p, c, q] = jnp.concatenate(half + half, axis=0).astype(BF)
    steer = jnp.concatenate(steer, axis=0).T
    turned = jnp.concatenate(turned, axis=0).T

    gains = part[pl.ds(index * 64 + 3, 16, stride=4), :].astype(BF)
    to_row = jnp.where((iota((512, 16), 0) & 15) == iota((512, 16), 1), 1.0, 0.0).astype(BF)
    spread = dot(to_row, gains)
    lane = iota((512, 128), 1)
    own_lane = lax.shift_right_logical(lane & 63, 1) == lax.shift_right_logical(iota((512, 128), 0), 4)
    spread = jnp.where(own_lane, spread, 0.0).astype(BF)
    source = iota((128, 256), 0)
    target = iota((128, 256), 1)
    fits = ((source & 1) == (lax.shift_right_logical(target, 6) & 1)) & (
        lax.shift_right_logical(source, 6) == lax.shift_right_logical(target, 7)
    )
    wide = dot(spread, jnp.where(fits, 1.0, 0.0).astype(BF))
    scaled = wide[:, 0:128] * steer + wide[:, 128:256] * turned
    hi, lo = split2(scaled)
    far_e[:, 0:128] = hi
    far_e[:, 128:256] = lo
    far_x = first.astype(BF)
    code = iota((8, 128), 0)
    lane = iota((8, 128), 1)
    fits = ((lane & 1) == (code & 1)) & (lax.shift_right_logical(lane, 6) == lax.shift_right_logical(code, 1))
    near_gain = dot_nt(jnp.where(fits, 1.0, 0.0).astype(BF), spread)

    for p in range(2):
        for half in range(2):
            cols = slice(half * 256, half * 256 + 256)
            sums = [jnp.zeros((8, 256), F32)] * 3
            for q in range(2):
                for r in range(4):
                    rows = slice(r * 128, r * 128 + 128)
                    vr = dot(far_x[rows], near_x[p, 0, q, :, cols])
                    vi = dot(far_x[rows], near_x[p, 1, q, :, cols])
                    ar = dot(far_e[rows, :], near_e[p, 0, q, :, cols])
                    ai = dot(far_e[rows, :], near_e[p, 1, q, :, cols])
                    mask = usable[rows, cols]
                    ur, ui = mask * ar, mask * ai
                    terms = (vr * ur - vi * ui, vr * ui + vi * ur, ur * ur + ui * ui)
                    sums = [s + jnp.sum(t.reshape(16, 8, 256), axis=0) for s, t in zip(sums, terms)]
            for n in range(3):
                acc[n, p, :, cols] = sums[n]

    steps = []
    for part_id in range(2):
        for p in range(2):
            weight_sum = jnp.sum(acc[2, p], axis=0, keepdims=True)
            moment = jnp.sum(acc[part_id, p], axis=0, keepdims=True) * (1.0 / NFRAMES)
            own = near_gain[part_id * 2 + p : part_id * 2 + p + 1]
            steps.append((moment - own * weight_sum) / (1.0 + weight_sum))

    mine = (iota((16, 512), 1) & 15) == iota((16, 512), 0)
    source = iota((512, 128), 0)
    target = iota((512, 128), 1)
    placed = jnp.zeros((48, 128), F32)
    for n, value in enumerate(steps):
        value = jnp.where(mine, jnp.broadcast_to(value, (16, 512)), 0.0)
        hi = value.astype(BF)
        rest = value - hi.astype(F32)
        mid = rest.astype(BF)
        low = (rest - mid.astype(F32)).astype(BF)
        column = (n // 2) * 64 + lax.shift_right_logical(source, 4) * 2 + (n % 2)
        move = jnp.where(target == column, 1.0, 0.0).astype(BF)
        placed = placed + dot(jnp.concatenate([hi, mid, low], axis=0), move)
    out_ref[...] = placed[0:16] + (placed[16:32] + placed[32:48])


def whole():
    return pl.BlockSpec(memory_space=pltpu.VMEM)


def make_spectra(index, volts, gains, flags):
    window, first, turn, second = filter_tables()
    return pl.pallas_call(
        spectra_kernel,
        out_shape=jax.ShapeDtypeStruct((4 * CW, 128), BF),
        in_specs=[pl.BlockSpec(memory_space=pltpu.SMEM)] + [whole()] * 7,
        out_specs=whole(),
        scratch_shapes=[pltpu.VMEM((32, 192, 128), BF), pltpu.VMEM((4 * CW, 128), F32)],
        compiler_params=pltpu.CompilerParams(vmem_limit_bytes=48 * 2**20),
        name="spectra",
    )(index, volts, jnp.asarray(window), jnp.asarray(first), jnp.asarray(turn), jnp.asarray(second), gains, flags)


def make_steps(index, recv, cos, sin, weights):
    return pl.pallas_call(
        pair_kernel,
        out_shape=jax.ShapeDtypeStruct((BLOCKS, 128), F32),
        in_specs=[pl.BlockSpec(memory_space=pltpu.SMEM)] + [whole()] * 4,
        out_specs=whole(),
        scratch_shapes=[
            pltpu.VMEM((4 * STATIONS, 128), F32),
            pltpu.VMEM((2, 2, 2, 128, STATIONS), BF),
            pltpu.VMEM((2, 2, 2, 256, STATIONS), BF),
            pltpu.VMEM((STATIONS, 256), BF),
            pltpu.VMEM((STATIONS, STATIONS), F32),
            pltpu.VMEM((3, 2, 8, STATIONS), F32),
        ],
        compiler_params=pltpu.CompilerParams(vmem_limit_bytes=48 * 2**20),
        name="pairs",
    )(index, recv, cos, sin, weights)


def steering_phases(positions, directions, channel):
    order = positions.reshape(BLOCKS, SPB, 2).transpose(2, 1, 0).reshape(2, STATIONS)
    delays = order[0][None, :] * directions[:, 0][:, None] + order[1][None, :] * directions[:, 1][:, None]
    scaled = 2.0 * math.pi * (1.0 + channel.astype(F32) / F)
    phases = scaled * delays
    return jnp.cos(phases), jnp.sin(phases)


def body(voltages, station_gains, positions, directions, weights, baseline_flags):
    chan_index = lax.axis_index("chan")
    stn_index = lax.axis_index("stn")
    index = jnp.reshape(chan_index, (1,)).astype(jnp.int32)
    channel = chan_index * BLOCKS + stn_index
    volts = voltages.reshape(2, FRAMES_IN, 64, 128)
    payload = make_spectra(index, volts, station_gains[:, 0, :], baseline_flags)
    recv = lax.all_to_all(
        payload.reshape(CW, 4, 128), ("chan", "stn"), split_axis=0, concat_axis=0, tiled=True
    )
    cos, sin = steering_phases(positions, directions, channel)
    steps = make_steps(index, recv.reshape(4 * CW, 128), cos, sin, weights)
    return lax.all_to_all(steps.reshape(BLOCKS, 1, 128), "stn", split_axis=0, concat_axis=0, tiled=True)


def solution(mesh):
    in_specs = (P("stn", "chan", None, None), P("chan", "stn", None), P(), P(), P(), P("stn", None))
    out_specs = P("chan", "stn", None)
    return jax.shard_map(body, mesh=mesh, in_specs=in_specs, out_specs=out_specs, check_vma=False)
```

time: 317 us -> 67 us (0.21)
  the two profiles are of different devices: /device:TPU:8 before, /device:TPU:1 now
where the time goes in v1:
time: 67 us; the launch traced here: 66.7 us
  starting transfers between devices  22.2 us (33%)
  waiting for transfers between devices  20.2 us (30%)
  blocking collectives  10.7 us (16%)
  Pallas kernels  8.72 us (13%)
  local copies, waits for them, and re-layouts  4.46 us (7%)
    all_to_all x1, starting transfers between devices, body(): lax.all_to_all(payload.reshape(CW, 4, 128), ('chan', 'stn'), split_axis=0...  22.2 us
    all_to_all x1, waiting for transfers between devices, body(): lax.all_to_all(payload.reshape(CW, 4, 128), ('chan', 'stn'), split_axis=0...  20.2 us
    all_to_all x1, blocking collectives, body(): lax.all_to_all(steps.reshape(BLOCKS, 1, 128), 'stn', split_axis=0, concat...  10.7 us
    pallas_call x1, Pallas kernels, make_spectra(): pl.pallas_call(spectra_kernel, out_shape=jax.ShapeDtypeStruct((4 * CW, 12...  4.97 us
    unnamed x21, local copies, waits for them, and re-layouts  4.14 us
    pallas_call x1, Pallas kernels, make_steps(): pl.pallas_call(pair_kernel, out_shape=jax.ShapeDtypeStruct((BLOCKS, 128),...  3.75 us
  transfers between devices with their start and end apart: 1, of which 1 were waited for; matrix products, arithmetic and copies ran while one was open for 1% of the time, Pallas kernels for 0%

profile of v1, /device:TPU:1, one launch (start us, length us, event | category | flops | bytes accessed | tf_op | source)
XLA Modules:
  0.0 66.7 jit_solution(17170428446205222519)
XLA Ops:
  0.0 0.0 copy-start.3
  0.0 0.0 copy-start.4
  0.0 1.4 %copy.19 = bf16[1,2,1984,128]{3,2,1,0:T(8,128)(2,1)S(1)} copy(bf16[1,2,1984,128]{3,1,2,0:T(2,128)(2,1)} %bitcast.22) | data formatting | bytes 2031616
  1.5 0.0 copy-start.5
  1.5 0.0 copy-done
  1.5 0.0 copy-done.1
  1.5 0.0 copy-done.2
  1.5 0.0 copy-done.3
  1.5 0.0 copy-done.4
  1.5 0.6 copy-done.5
  2.2 5.0 %spectra.1 = bf16[2048,128]{1,0:T(8,128)(2,1)} custom-call(s32[1]{0:T(128)} %bitcast.index_ref, bf16[2,31,64,128]{3,2,1,0:T(8,128)(2,1)S(1)} %bitcast.18, f32[16,64,128]{2,1,0:T(8,128)S(1)} %copy-done, bf16[128,192]{1,0:T(8,128)(2,1)S(1)} %copy-done.3, f32[2,64,128]{2,1,0:T(8,128)S(1)} %copy-done.4, bf16[2,256,256]{2,1,0:T(8,128)(2,1)S(1)} %copy-done.1, ...), custom_call_target="tpu_custom_call" | custom-call | tf_op jit(solution)/shard_map/spectra/pallas_call | solution.py:263
  7.1 22.2 %all-to-all-start = ((bf16[512,4,128]{2,1,0:T(4,128)(2,1)}), bf16[512,4,128]{2,1,0:T(4,128)(2,1)S(1)}, u32[]{:S(2)}, u32[]{:S(2)}) async-start(bf16[512,4,128]{2,1,0:T(4,128)(2,1)} %bitcast.2), calls=%async_computation | async-start | bytes 1048576 | tf_op jit(solution)/shard_map/all_to_all | solution.py:308
  29.3 0.1 reshape.27
  29.4 0.1 copy.16
  29.5 0.1 mul.50
  29.6 0.1 mul.45
  29.6 0.7 %copy-done.7 = f32[32,2]{0,1:T(2,128)S(1)} copy-done((f32[32,2]{0,1:T(2,128)S(1)}, f32[32,2]{0,1:T(2,128)}, u32[]{:S(2)}) %copy-start.7) | copy-done | bytes 280
  30.3 0.1 copy.17.weight_ref
  30.4 0.7 %copy-done.8 = f32[32,2]{0,1:T(2,128)S(1)} copy-done((f32[32,2]{0,1:T(2,128)S(1)}, f32[32,2]{0,1:T(2,128)}, u32[]{:S(2)}) %copy-start.8) | copy-done | bytes 280
  31.1 0.3 fusion
  31.4 20.2 %all-to-all-done = bf16[512,4,128]{2,1,0:T(4,128)(2,1)S(1)} async-done(((bf16[512,4,128]{2,1,0:T(4,128)(2,1)}), bf16[512,4,128]{2,1,0:T(4,128)(2,1)S(1)}, u32[]{:S(2)}, u32[]{:S(2)}) %all-to-all-start) | async-done | bytes 524320 | tf_op jit(solution)/shard_map/all_to_all | solution.py:308
  51.6 3.8 %pairs.1 = f32[16,128]{1,0:T(8,128)S(1)} custom-call(s32[1]{0:T(128)} %bitcast.index_ref, bf16[2048,128]{1,0:T(8,128)(2,1)S(1)} %bitcast.19, f32[32,512]{1,0:T(8,128)S(1)} %get-tuple-element.8.cos_ref, f32[32,512]{1,0:T(8,128)S(1)} %get-tuple-element.7.sin_ref, f32[32,2]{1,0:T(8,128)S(1)} %copy.17.weight_ref), custom_call_target="tpu_custom_call" | custom-call | tf_op jit(solution)/shard_map/pairs/pallas_call | solution.py:275
  55.4 10.7 %all_to_all.10 = f32[16,1,128]{2,1,0:T(1,128)S(1)} all-to-all(f32[16,1,128]{2,1,0:T(1,128)S(1)} %bitcast.20), channel_id=1, replica_groups=mesh['chan'=32,'stn'=16] {'stn'}, dimensions={0} | all-to-all | bytes 16384 | tf_op jit(solution)/shard_map/all_to_all | solution.py:313
  66.1 0.6 copy.21
  (9 shorter events, 0.0 us)
Async XLA Ops:
  0.0 1.5 %copy-start = (f32[16,64,128]{2,1,0:T(8,128)S(1)}, f32[16,64,128]{2,1,0:T(8,128)}, u32[]{:S(2)}) copy-start(f32[16,64,128]{2,1,0:T(8,128)} %constant.26.clone.win_ref) | copy-start | bytes 1572868
  0.0 1.5 %copy-start.1 = (bf16[2,256,256]{2,1,0:T(8,128)(2,1)S(1)}, bf16[2,256,256]{2,1,0:T(8,128)(2,1)}, u32[]{:S(2)}) copy-start(bf16[2,256,256]{2,1,0:T(8,128)(2,1)} %constant.29.clone.second_ref) | copy-start | bytes 786436
  0.0 1.5 %copy-start.2 = (s32[32,512]{1,0:T(8,128)S(1)}, s32[32,512]{1,0:T(8,128)}, u32[]{:S(2)}) copy-start(s32[32,512]{1,0:T(8,128)} %flag_ref.1) | copy-start | bytes 196612
  0.0 1.5 %copy-start.3 = (bf16[128,192]{1,0:T(8,128)(2,1)S(1)}, bf16[128,192]{1,0:T(8,128)(2,1)}, u32[]{:S(2)}) copy-start(bf16[128,192]{1,0:T(8,128)(2,1)} %constant.27.clone.first_ref) | copy-start | bytes 147460
  0.0 1.5 %copy-start.4 = (f32[2,64,128]{2,1,0:T(8,128)S(1)}, f32[2,64,128]{2,1,0:T(8,128)}, u32[]{:S(2)}) copy-start(f32[2,64,128]{2,1,0:T(8,128)} %constant.28.clone.turn_ref) | copy-start | bytes 196612
  1.5 0.7 %copy-start.5 = (bf16[16,1,128]{2,0,1:T(8,128)(2,1)S(1)}, bf16[16,1,128]{2,0,1:T(8,128)(2,1)}, u32[]{:S(2)}) copy-start(bf16[16,1,128]{2,0,1:T(8,128)(2,1)} %param.11) | copy-start | bytes 12292
  7.1 22.2 %copy-start.6 = (f32[512,2]{0,1:T(2,128)S(1)}, f32[512,2]{0,1:T(2,128)}, u32[]{:S(2)}) copy-start(f32[512,2]{0,1:T(2,128)} %param.12) | copy-start | bytes 12292
  7.1 44.5 %all-to-all-start = ((bf16[512,4,128]{2,1,0:T(4,128)(2,1)}), bf16[512,4,128]{2,1,0:T(4,128)(2,1)S(1)}, u32[]{:S(2)}, u32[]{:S(2)}) async-start(bf16[512,4,128]{2,1,0:T(4,128)(2,1)} %bitcast.2), calls=%async_computation | async-start | bytes 1048576 | tf_op jit(solution)/shard_map/all_to_all | solution.py:308
  29.6 0.7 %copy-start.7 = (f32[32,2]{0,1:T(2,128)S(1)}, f32[32,2]{0,1:T(2,128)}, u32[]{:S(2)}) copy-start(f32[32,2]{0,1:T(2,128)} %param.14) | copy-start | bytes 772
  30.4 0.7 %copy-start.8 = (f32[32,2]{0,1:T(2,128)S(1)}, f32[32,2]{0,1:T(2,128)}, u32[]{:S(2)}) copy-start(f32[32,2]{0,1:T(2,128)} %param.13) | copy-start | bytes 772

commit v2 on v1

v2 whole, which is shorter than its diff:
```python
import math

import jax
import jax.numpy as jnp
import numpy as np
from jax import lax
from jax.experimental import pallas as pl
from jax.experimental.pallas import tpu as pltpu
from jax.sharding import PartitionSpec as P

F = 4096
CW = 512
FRAME = 8192
TAPS = 16
STATIONS = 512
NFRAMES = 16
SOURCES = 32
BLOCKS = 16
SPB = 32
FRAMES_IN = NFRAMES + TAPS - 1
CHUNKS = 8
CHUNK = 16
ROWS = 256
BF = jnp.bfloat16
F32 = jnp.float32


def split_np(values):
    hi = values.astype(jnp.bfloat16)
    lo = (values - hi.astype(np.float64)).astype(jnp.bfloat16)
    return hi, lo


def filter_tables():
    n = np.arange(TAPS * FRAME, dtype=np.float64)
    q = (n + 0.5 - TAPS * FRAME / 2) / FRAME
    window = np.sin(np.pi * q) / (np.pi * q) * (0.5 - 0.5 * np.cos(2 * np.pi * n / (TAPS * FRAME)))
    window = window.astype(np.float32).reshape(TAPS, 64, 128)
    window = np.repeat(window, 2, axis=1).reshape(TAPS, CHUNKS, 16, 128).transpose(1, 0, 2, 3)
    j = np.arange(64)[:, None]
    k = np.arange(64)[None, :]
    angle = 2 * np.pi * (k * j % 64) / 64
    first = np.stack([np.cos(angle), -np.sin(angle)])
    first = np.einsum("cjk,st->jsctk", first, np.eye(2)).reshape(128, 256)
    hi, lo = split_np(first)
    first = np.concatenate([hi, hi, lo], axis=0)
    m = np.arange(128)[:, None]
    angle = 2 * np.pi * (k * m % 8192) / 8192
    turn = np.stack([np.cos(angle), np.sin(angle)])
    turn = np.concatenate([turn, turn], axis=2).astype(np.float32)
    b = np.arange(8)[:, None]
    m = np.arange(128)[None, :]
    angle = 2 * np.pi * (b * m % 128) / 128
    c = np.cos(angle) / math.sqrt(FRAME)
    s = np.sin(angle) / math.sqrt(FRAME)
    to_re = np.concatenate([c, s], axis=1)
    to_im = np.concatenate([-s, c], axis=1)
    second = np.stack([to_re, to_im], axis=1).reshape(16, 256)
    second = np.concatenate(split_np(second), axis=0)
    return window, first, turn, second


def split2(x):
    hi = x.astype(BF)
    return hi, (x - hi.astype(F32)).astype(BF)


def dot(a, b):
    return lax.dot_general(a, b, (((1,), (0,)), ((), ())), preferred_element_type=F32)


def dot_nt(a, b):
    return lax.dot_general(a, b, (((1,), (1,)), ((), ())), preferred_element_type=F32)


def iota(shape, dim):
    return lax.broadcasted_iota(jnp.int32, shape, dim)


def spectra_kernel(
    index_ref,
    volt_ref,
    win_ref,
    first_ref,
    turn_ref,
    second_ref,
    gain_ref,
    flag_ref,
    out_ref,
    volts,
    window,
    first,
    turn,
    second,
    gain,
    flag,
    fold,
    gathered,
    part,
    ready,
    sems,
    late,
    left,
    section,
    high,
    low,
):

    def volt_copy(step):
        rows = pl.ds(pl.multiple_of(step * 16, 16), 16)
        return pltpu.make_async_copy(volt_ref.at[:, rows, :], volts.at[step], sems.at[0, step])

    def window_copy(step):
        return pltpu.make_async_copy(win_ref.at[step], window.at[step], sems.at[1, step])

    early = [
        pltpu.make_async_copy(source, target, late.at[n])
        for n, (source, target) in enumerate(((gain_ref, gain), (flag_ref, flag)))
    ]
    others = [
        pltpu.make_async_copy(source, target, late.at[n + 2])
        for n, (source, target) in enumerate(((first_ref, first), (turn_ref, turn), (second_ref, second)))
    ]
    volt_copy(0).start()
    window_copy(0).start()
    for copy in early:
        copy.start()
    for step in range(1, CHUNKS):
        volt_copy(step).start()
        window_copy(step).start()
    for copy in others:
        copy.start()

    index = index_ref[0]
    place = (iota((1, 384), 1) + 64 * (index // 4)) & (STATIONS - 1)
    wanted = (place & 15) * SPB + lax.shift_right_logical(place, 4)
    pick = jnp.where(iota((STATIONS, 384), 0) == wanted, 1.0, 0.0).astype(BF)
    for copy in early:
        copy.wait()
    flags = jnp.broadcast_to(flag[pl.ds(index, 1), :].astype(F32), (8, STATIONS)).astype(BF)
    row = dot(flags, pick)[0:1]
    part[pl.ds(1, 512, stride=4), :] = jnp.broadcast_to(row[:, 64:192], (512, 128))
    part[pl.ds(2, 512, stride=4), :] = jnp.broadcast_to(row[:, 192:320], (512, 128))
    gains = gain[...].astype(F32)
    for i in range(32):
        part[pl.ds(i * 64 + 3, 16, stride=4), :] = gains

    def chunk(step, carry):
        volt_copy(step).wait()
        window_copy(step).wait()
        x = volts[step].astype(F32)
        acc = x[0:NFRAMES] * window[step, 0][None]
        for tap in range(1, TAPS):
            acc = acc + x[tap : tap + NFRAMES] * window[step, tap][None]
        fold[:, pl.ds(pl.multiple_of(step * 16, 16), 16), :] = acc
        return carry

    lax.fori_loop(0, CHUNKS, chunk, 0)
    for copy in others:
        copy.wait()

    turn_cos = turn[0]
    turn_sin = turn[1]
    for t in range(NFRAMES):
        hi, lo = split2(fold[t].T)
        rows = slice(t * 128, t * 128 + 128)
        left[rows, 0:128] = hi
        left[rows, 128:256] = lo
    for group in range(4):
        rows = slice(group * 512, group * 512 + 512)
        section[rows, :] = dot(left[rows, :], first[0:256]) + dot(left[rows, 0:128], first[256:384])
    for t in range(NFRAMES):
        rows = slice(t * 128, t * 128 + 128)
        re = section[rows, 0:128]
        im = section[rows, 128:256]
        for part_id, value in enumerate((re * turn_cos + im * turn_sin, im * turn_cos - re * turn_sin)):
            hi, lo = split2(value)
            place = slice(part_id * 128, part_id * 128 + 128)
            high[place, rows] = hi
            low[place, rows] = lo
    main = dot(second[...], high[...])
    rest = dot(second[0:16], low[...])
    value = main[0:16] + (main[16:32] + rest)
    for t in range(NFRAMES):
        gathered[pl.ds(t, 16, stride=16), :] = value[:, t * 128 : t * 128 + 128]
    total = gathered[...].T

    copies = []
    for b in range(8):
        lanes = [
            total[0:64, b * 32 : b * 32 + 32],
            total[64:128, b * 32 : b * 32 + 32],
            jnp.broadcast_to(row[:, 0:64], (64, 64)),
        ]
        rows = pl.ds(b * 256, 256)
        part[pl.ds(b * 256, 64, stride=4), :] = jnp.concatenate(lanes, axis=1)
        ready[rows, :] = part[rows, :].astype(BF)
        copies.append(pltpu.make_async_copy(ready.at[rows, :], out_ref.at[rows, :], sems.at[0, b]))
        copies[-1].start()
    for copy in copies:
        copy.wait()


def steer_kernel(cos_ref, sin_ref, weight_ref, near_e, steer_ref, turned_ref):
    cos, sin = cos_ref[...], sin_ref[...]
    steer, turned = [], []
    for p in range(2):
        weight = weight_ref[:, p : p + 1]
        re = (cos * weight).astype(BF).astype(F32)
        im = (-sin * weight).astype(BF).astype(F32)
        steer += [re, im]
        turned += [-im, re]
        near_e[p, 0] = jnp.concatenate([re, im, re, im], axis=0).astype(BF)
        near_e[p, 1] = jnp.concatenate([-im, re, -im, re], axis=0).astype(BF)
    steer_ref[...] = jnp.concatenate(steer, axis=0).T
    turned_ref[...] = jnp.concatenate(turned, axis=0).T


def pair_kernel(
    index_ref, recv_ref, near_e, steer_ref, turned_ref, out_ref, part, near_x, far_x, far_e, usable, acc, *products
):
    part[...] = recv_ref[...].astype(F32)
    first = part[pl.ds(0, 512, stride=4), :]
    index = index_ref[0]

    sent = jnp.concatenate(
        [
            first[:, 64:128],
            part[pl.ds(1, 512, stride=4), :],
            part[pl.ds(2, 512, stride=4), :],
        ],
        axis=1,
    )
    empty = jnp.zeros((64, 64), F32)
    for a in range(8):
        pieces = []
        for b in range(8):
            d = (b - a) % 8
            pieces.append(sent[a * 64 : a * 64 + 64, d * 64 : d * 64 + 64] if d <= 4 else empty)
        usable[pl.ds(a * 64, 64), :] = jnp.concatenate(pieces, axis=1)
    brought = usable[...]
    rows, cols = iota((512, 512), 0), iota((512, 512), 1)
    ahead = (lax.shift_right_logical(cols, 6) - lax.shift_right_logical(rows, 6)) & 7
    both = jnp.where(ahead <= 4, brought, brought.T)
    usable[...] = jnp.where(rows == cols, 0.0, both)

    xt = first.T
    for p in range(2):
        own = xt[p * 32 : p * 32 + 32]
        near_x[p, 0] = own.astype(BF)
        near_x[p, 1] = jnp.concatenate([own[16:32], -own[0:16]], axis=0).astype(BF)
        far_x[p] = first[:, p * 32 : p * 32 + 32].astype(BF)

    gains = part[pl.ds(index * 64 + 3, 16, stride=4), :].astype(BF)
    to_row = jnp.where((iota((512, 16), 0) & 15) == iota((512, 16), 1), 1.0, 0.0).astype(BF)
    spread = dot(to_row, gains)
    lane = iota((512, 128), 1)
    own_lane = lax.shift_right_logical(lane & 63, 1) == lax.shift_right_logical(iota((512, 128), 0), 4)
    spread = jnp.where(own_lane, spread, 0.0).astype(BF)
    source = iota((128, 256), 0)
    target = iota((128, 256), 1)
    fits = ((source & 1) == (lax.shift_right_logical(target, 6) & 1)) & (
        lax.shift_right_logical(source, 6) == lax.shift_right_logical(target, 7)
    )
    wide = dot(spread, jnp.where(fits, 1.0, 0.0).astype(BF))
    scaled = wide[:, 0:128] * steer_ref[...] + wide[:, 128:256] * turned_ref[...]
    for q in range(2):
        hi, lo = split2(scaled[:, q * 64 : q * 64 + 64])
        far_e[q] = jnp.concatenate([hi, lo], axis=1)
    code = iota((8, 128), 0)
    lane = iota((8, 128), 1)
    fits = ((lane & 1) == (code & 1)) & (lax.shift_right_logical(lane, 6) == lax.shift_right_logical(code, 1))
    near_gain = dot_nt(jnp.where(fits, 1.0, 0.0).astype(BF), spread)

    blocks = [(p, half, q) for p in range(2) for half in range(2) for q in range(2)]
    sums = {}
    for n in range(len(blocks) + 1):
        for r in range(0, STATIONS, ROWS):
            rows = slice(r, r + ROWS)
            if n < len(blocks):
                p, half, q = blocks[n]
                cols = slice(half * 256, half * 256 + 256)
                vr, vi, ar, ai = products[4 * (n % 2) : 4 * (n % 2) + 4]
                vr[rows, :] = dot(far_x[q, rows], near_x[p, 0, :, cols])
                vi[rows, :] = dot(far_x[q, rows], near_x[p, 1, :, cols])
                ar[rows, :] = dot(far_e[q, rows], near_e[p, 0, :, cols])
                ai[rows, :] = dot(far_e[q, rows], near_e[p, 1, :, cols])
            if n > 0:
                p, half, q = blocks[n - 1]
                cols = slice(half * 256, half * 256 + 256)
                vr, vi, ar, ai = products[4 * ((n - 1) % 2) : 4 * ((n - 1) % 2) + 4]
                total = sums.get((p, half), [jnp.zeros((8, 256), F32)] * 3)
                for c in range(r, r + ROWS, CHUNK):
                    some = slice(c, c + CHUNK)
                    mask = usable[some, cols]
                    ur, ui = mask * ar[some, :], mask * ai[some, :]
                    xr, xi = vr[some, :], vi[some, :]
                    terms = (xr * ur - xi * ui, xr * ui + xi * ur, ur * ur + ui * ui)
                    total = [s + jnp.sum(t.reshape(CHUNK // 8, 8, 256), axis=0) for s, t in zip(total, terms)]
                sums[p, half] = total
    for (p, half), total in sums.items():
        for n in range(3):
            acc[n, p, :, half * 256 : half * 256 + 256] = total[n]

    steps = []
    for part_id in range(2):
        for p in range(2):
            weight_sum = jnp.sum(acc[2, p], axis=0, keepdims=True)
            moment = jnp.sum(acc[part_id, p], axis=0, keepdims=True) * (1.0 / NFRAMES)
            own = near_gain[part_id * 2 + p : part_id * 2 + p + 1]
            steps.append((moment - own * weight_sum) / (1.0 + weight_sum))

    mine = (iota((16, 512), 1) & 15) == iota((16, 512), 0)
    source = iota((512, 128), 0)
    target = iota((512, 128), 1)
    placed = jnp.zeros((48, 128), F32)
    for n, value in enumerate(steps):
        value = jnp.where(mine, jnp.broadcast_to(value, (16, 512)), 0.0)
        hi = value.astype(BF)
        rest = value - hi.astype(F32)
        mid = rest.astype(BF)
        low = (rest - mid.astype(F32)).astype(BF)
        column = (n // 2) * 64 + lax.shift_right_logical(source, 4) * 2 + (n % 2)
        move = jnp.where(target == column, 1.0, 0.0).astype(BF)
        placed = placed + dot(jnp.concatenate([hi, mid, low], axis=0), move)
    out_ref[...] = placed[0:16] + (placed[16:32] + placed[32:48])


def whole():
    return pl.BlockSpec(memory_space=pltpu.VMEM)


def anywhere():
    return pl.BlockSpec(memory_space=pltpu.HBM)


def make_spectra(index, volts, gains, flags):
    window, first, turn, second = filter_tables()
    return pl.pallas_call(
        spectra_kernel,
        out_shape=jax.ShapeDtypeStruct((4 * CW, 128), BF),
        in_specs=[pl.BlockSpec(memory_space=pltpu.SMEM)] + [anywhere()] * 7,
        out_specs=anywhere(),
        scratch_shapes=[
            pltpu.VMEM((CHUNKS, FRAMES_IN, 16, 128), BF),
            pltpu.VMEM((CHUNKS, TAPS, 16, 128), F32),
            pltpu.VMEM((384, 256), BF),
            pltpu.VMEM((2, 128, 128), F32),
            pltpu.VMEM((32, 256), BF),
            pltpu.VMEM((BLOCKS, 128), BF),
            pltpu.VMEM((SPB, STATIONS), jnp.int32),
            pltpu.VMEM((NFRAMES, 128, 128), F32),
            pltpu.VMEM((256, 128), F32),
            pltpu.VMEM((4 * CW, 128), F32),
            pltpu.VMEM((4 * CW, 128), BF),
            pltpu.SemaphoreType.DMA((2, CHUNKS)),
            pltpu.SemaphoreType.DMA((5,)),
            pltpu.VMEM((NFRAMES * 128, 256), BF),
            pltpu.VMEM((NFRAMES * 128, 256), F32),
            pltpu.VMEM((256, NFRAMES * 128), BF),
            pltpu.VMEM((256, NFRAMES * 128), BF),
        ],
        compiler_params=pltpu.CompilerParams(vmem_limit_bytes=60 * 2**20),
        name="spectra",
    )(index, volts, jnp.asarray(window), jnp.asarray(first), jnp.asarray(turn), jnp.asarray(second), gains, flags)


def arrange(voltages):
    rows = voltages.reshape(2, FRAMES_IN * 64, 128).transpose(1, 0, 2)
    return rows.reshape(FRAMES_IN, 128, 128)


def make_steering(cos, sin, weights):
    return pl.pallas_call(
        steer_kernel,
        out_shape=(
            jax.ShapeDtypeStruct((2, 2, 128, STATIONS), BF),
            jax.ShapeDtypeStruct((STATIONS, 128), F32),
            jax.ShapeDtypeStruct((STATIONS, 128), F32),
        ),
        in_specs=[whole()] * 3,
        out_specs=(whole(),) * 3,
        compiler_params=pltpu.CompilerParams(vmem_limit_bytes=16 * 2**20),
        name="steer",
    )(cos, sin, weights)


def make_steps(index, recv, near_e, steer, turned):
    return pl.pallas_call(
        pair_kernel,
        out_shape=jax.ShapeDtypeStruct((BLOCKS, 128), F32),
        in_specs=[pl.BlockSpec(memory_space=pltpu.SMEM)] + [whole()] * 4,
        out_specs=whole(),
        scratch_shapes=[
            pltpu.VMEM((4 * STATIONS, 128), F32),
            pltpu.VMEM((2, 2, 32, STATIONS), BF),
            pltpu.VMEM((2, STATIONS, 32), BF),
            pltpu.VMEM((2, STATIONS, 128), BF),
            pltpu.VMEM((STATIONS, STATIONS), F32),
            pltpu.VMEM((3, 2, 8, STATIONS), F32),
        ]
        + [pltpu.VMEM((STATIONS, 256), F32)] * 8,
        compiler_params=pltpu.CompilerParams(vmem_limit_bytes=24 * 2**20),
        name="pairs",
    )(index, recv, near_e, steer, turned)


def steering_phases(positions, directions, channel):
    order = positions.reshape(BLOCKS, SPB, 2).transpose(2, 1, 0).reshape(2, STATIONS)
    delays = order[0][None, :] * directions[:, 0][:, None] + order[1][None, :] * directions[:, 1][:, None]
    scaled = 2.0 * math.pi * (1.0 + channel.astype(F32) / F)
    phases = scaled * delays
    return jnp.cos(phases), jnp.sin(phases)


def body(voltages, station_gains, positions, directions, weights, baseline_flags):
    chan_index = lax.axis_index("chan")
    stn_index = lax.axis_index("stn")
    index = jnp.reshape(chan_index, (1,)).astype(jnp.int32)
    channel = chan_index * BLOCKS + stn_index
    volts = arrange(voltages)
    payload = make_spectra(index, volts, station_gains[:, 0, :], baseline_flags)
    recv = lax.all_to_all(
        payload.reshape(CW, 4, 128), ("chan", "stn"), split_axis=0, concat_axis=0, tiled=True
    )
    cos, sin = steering_phases(positions, directions, channel)
    steps = make_steps(index, recv.reshape(4 * CW, 128), *make_steering(cos, sin, weights))
    return lax.all_to_all(steps.reshape(BLOCKS, 1, 128), "stn", split_axis=0, concat_axis=0, tiled=True)


def solution(mesh):
    in_specs = (P("stn", "chan", None, None), P("chan", "stn", None), P(), P(), P(), P("stn", None))
    out_specs = P("chan", "stn", None)
    return jax.shard_map(body, mesh=mesh, in_specs=in_specs, out_specs=out_specs, check_vma=False)
```

time: 67 us -> 65.5 us (0.978)
  local copies, waits for them, and re-layouts: 4.46 us -> 2.97 us
  Pallas kernels: 8.72 us -> 9.63 us
  waiting for transfers between devices: 20.2 us -> 19.4 us
    unnamed x21 -> x8, local copies, waits for them, and re-layouts: 4.14 us -> 2.65 us
    all_to_all x1, waiting for transfers between devices: 20.2 us -> 19.4 us  [body(): lax.all_to_all(payload.reshape(CW, 4, 128), ('chan', 'stn'), split_axis=0...]
    pallas_call x1, Pallas kernels: 4.97 us -> 5.76 us  [make_spectra(): pl.pallas_call(spectra_kernel, out_shape=jax.ShapeDtypeStruct((4 * CW, 12...]
where the time goes in v2:
time: 65.5 us; the launch traced here: 65.2 us
  starting transfers between devices  22.2 us (34%)
  waiting for transfers between devices  19.4 us (30%)
  blocking collectives  10.7 us (16%)
  Pallas kernels  9.63 us (15%)
  local copies, waits for them, and re-layouts  2.97 us (5%)
    all_to_all x1, starting transfers between devices, body(): lax.all_to_all(payload.reshape(CW, 4, 128), ('chan', 'stn'), split_axis=0...  22.2 us
    all_to_all x1, waiting for transfers between devices, body(): lax.all_to_all(payload.reshape(CW, 4, 128), ('chan', 'stn'), split_axis=0...  19.4 us
    all_to_all x1, blocking collectives, body(): lax.all_to_all(steps.reshape(BLOCKS, 1, 128), 'stn', split_axis=0, concat...  10.7 us
    pallas_call x1, Pallas kernels, make_spectra(): pl.pallas_call(spectra_kernel, out_shape=jax.ShapeDtypeStruct((4 * CW, 12...  5.76 us
    pallas_call x1, Pallas kernels, make_steps(): pl.pallas_call(pair_kernel, out_shape=jax.ShapeDtypeStruct((BLOCKS, 128),...  3.62 us
    unnamed x8, local copies, waits for them, and re-layouts  2.65 us
  transfers between devices with their start and end apart: 1, of which 1 were waited for; matrix products, arithmetic and copies ran while one was open for 1% of the time, Pallas kernels for 0%

profile of v2, /device:TPU:1, one launch (start us, length us, event | category | flops | bytes accessed | tf_op | source)
XLA Modules:
  0.0 65.2 jit_solution(14692408418731376664)
XLA Ops:
  0.0 5.8 %spectra.1 = bf16[2048,128]{1,0:T(8,128)(2,1)} custom-call(s32[1]{0:T(128)} %bitcast.index_ref, bf16[31,128,128]{2,1,0:T(8,128)(2,1)} %bitcast.22, f32[8,16,16,128]{3,2,1,0:T(8,128)} %constant.26.clone.win_ref, bf16[384,256]{1,0:T(8,128)(2,1)} %constant.27.clone.first_ref, f32[2,128,128]{2,1,0:T(8,128)} %constant.28.clone.turn_ref, ...), custom_call_target="tpu_custom_call" | custom-call | tf_op jit(solution)/shard_map/spectra/pallas_call | solution.py:339
  5.8 22.2 %all-to-all-start = ((bf16[512,4,128]{2,1,0:T(4,128)(2,1)}), bf16[512,4,128]{2,1,0:T(4,128)(2,1)S(1)}, u32[]{:S(2)}, u32[]{:S(2)}) async-start(bf16[512,4,128]{2,1,0:T(4,128)(2,1)} %bitcast.21), calls=%async_computation | async-start | bytes 1048576 | tf_op jit(solution)/shard_map/all_to_all | solution.py:423
  27.9 0.0 copy-start
  28.0 0.7 %copy-done = f32[512,2]{0,1:T(2,128)S(1)} copy-done((f32[512,2]{0,1:T(2,128)S(1)}, f32[512,2]{0,1:T(2,128)}, u32[]{:S(2)}) %copy-start) | copy-done | bytes 4120
  28.6 0.1 reshape.31
  28.7 0.1 copy.19
  28.8 0.1 mul.45
  28.9 0.0 copy-start.1
  28.9 0.1 mul.50
  29.0 0.6 copy-done.1
  29.6 0.1 copy.20.weight_ref
  29.7 0.0 copy-start.2
  29.7 0.7 %copy-done.2 = f32[32,2]{0,1:T(2,128)S(1)} copy-done((f32[32,2]{0,1:T(2,128)S(1)}, f32[32,2]{0,1:T(2,128)}, u32[]{:S(2)}) %copy-start.2) | copy-done | bytes 280
  30.3 0.3 fusion
  30.7 0.3 steer.1
  30.9 19.4 %all-to-all-done = bf16[512,4,128]{2,1,0:T(4,128)(2,1)S(1)} async-done(((bf16[512,4,128]{2,1,0:T(4,128)(2,1)}), bf16[512,4,128]{2,1,0:T(4,128)(2,1)S(1)}, u32[]{:S(2)}, u32[]{:S(2)}) %all-to-all-start) | async-done | bytes 524320 | tf_op jit(solution)/shard_map/all_to_all | solution.py:423
  50.3 3.6 %pairs.1 = f32[16,128]{1,0:T(8,128)S(1)} custom-call(s32[1]{0:T(128)} %bitcast.index_ref, bf16[2048,128]{1,0:T(8,128)(2,1)S(1)} %bitcast.19, bf16[2,2,128,512]{3,2,1,0:T(8,128)(2,1)S(1)} %get-tuple-element.8.near_e, f32[512,128]{1,0:T(8,128)S(1)} %get-tuple-element.9.steer_ref, f32[512,128]{1,0:T(8,128)S(1)} %get-tuple-element.10.turned_ref), custom_call_target="tpu_custom_call" | custom-call | tf_op jit(solution)/shard_map/pairs/pallas_call | solution.py:389
  53.9 10.7 %all_to_all.10 = f32[16,1,128]{2,1,0:T(1,128)S(1)} all-to-all(f32[16,1,128]{2,1,0:T(1,128)S(1)} %bitcast.20), channel_id=1, replica_groups=mesh['chan'=32,'stn'=16] {'stn'}, dimensions={0} | all-to-all | bytes 16384 | tf_op jit(solution)/shard_map/all_to_all | solution.py:428
  64.6 0.6 copy.23
  (2 shorter events, 0.0 us)
Async XLA Ops:
  5.8 44.5 %all-to-all-start = ((bf16[512,4,128]{2,1,0:T(4,128)(2,1)}), bf16[512,4,128]{2,1,0:T(4,128)(2,1)S(1)}, u32[]{:S(2)}, u32[]{:S(2)}) async-start(bf16[512,4,128]{2,1,0:T(4,128)(2,1)} %bitcast.21), calls=%async_computation | async-start | bytes 1048576 | tf_op jit(solution)/shard_map/all_to_all | solution.py:423
  27.9 0.7 %copy-start = (f32[512,2]{0,1:T(2,128)S(1)}, f32[512,2]{0,1:T(2,128)}, u32[]{:S(2)}) copy-start(f32[512,2]{0,1:T(2,128)} %param.12) | copy-start | bytes 12292
  28.9 0.7 %copy-start.1 = (f32[32,2]{0,1:T(2,128)S(1)}, f32[32,2]{0,1:T(2,128)}, u32[]{:S(2)}) copy-start(f32[32,2]{0,1:T(2,128)} %param.14) | copy-start | bytes 772
  29.7 0.7 %copy-start.2 = (f32[32,2]{0,1:T(2,128)S(1)}, f32[32,2]{0,1:T(2,128)}, u32[]{:S(2)}) copy-start(f32[32,2]{0,1:T(2,128)} %param.13) | copy-start | bytes 772

commit v3 on v2

--- a/solution.py
+++ b/solution.py
@@ -6,6 +6,7 @@
 from jax import lax
 from jax.experimental import pallas as pl
 from jax.experimental.pallas import tpu as pltpu
+from jax.sharding import Mesh
 from jax.sharding import PartitionSpec as P
 
 F = 4096
@@ -21,6 +22,8 @@
 CHUNKS = 8
 CHUNK = 16
 ROWS = 256
+CHAN = ("y", "z_hi", "core")
+STN = ("x", "z_lo")
 BF = jnp.bfloat16
 F32 = jnp.float32
 
@@ -78,34 +81,26 @@
 
 
 def spectra_kernel(
-    index_ref,
     volt_ref,
     win_ref,
     first_ref,
     turn_ref,
     second_ref,
-    gain_ref,
-    flag_ref,
     out_ref,
     volts,
     window,
     first,
     turn,
     second,
-    gain,
-    flag,
     fold,
-    gathered,
-    part,
-    ready,
-    sems,
-    late,
     left,
     section,
     high,
     low,
+    gathered,
+    sems,
+    late,
 ):
-
     def volt_copy(step):
         rows = pl.ds(pl.multiple_of(step * 16, 16), 16)
         return pltpu.make_async_copy(volt_ref.at[:, rows, :], volts.at[step], sems.at[0, step])
@@ -113,37 +108,17 @@
     def window_copy(step):
         return pltpu.make_async_copy(win_ref.at[step], window.at[step], sems.at[1, step])
 
-    early = [
+    others = [
         pltpu.make_async_copy(source, target, late.at[n])
-        for n, (source, target) in enumerate(((gain_ref, gain), (flag_ref, flag)))
+        for n, (source, target) in enumerate(
+            ((first_ref, first), (turn_ref, turn), (second_ref, second))
+        )
     ]
-    others = [
-        pltpu.make_async_copy(source, target, late.at[n + 2])
-        for n, (source, target) in enumerate(((first_ref, first), (turn_ref, turn), (second_ref, second)))
-    ]
-    volt_copy(0).start()
-    window_copy(0).start()
-    for copy in early:
-        copy.start()
-    for step in range(1, CHUNKS):
+    for step in range(CHUNKS):
         volt_copy(step).start()
         window_copy(step).start()
     for copy in others:
         copy.start()
-
-    index = index_ref[0]
-    place = (iota((1, 384), 1) + 64 * (index // 4)) & (STATIONS - 1)
-    wanted = (place & 15) * SPB + lax.shift_right_logical(place, 4)
-    pick = jnp.where(iota((STATIONS, 384), 0) == wanted, 1.0, 0.0).astype(BF)
-    for copy in early:
-        copy.wait()
-    flags = jnp.broadcast_to(flag[pl.ds(index, 1), :].astype(F32), (8, STATIONS)).astype(BF)
-    row = dot(flags, pick)[0:1]
-    part[pl.ds(1, 512, stride=4), :] = jnp.broadcast_to(row[:, 64:192], (512, 128))
-    part[pl.ds(2, 512, stride=4), :] = jnp.broadcast_to(row[:, 192:320], (512, 128))
-    gains = gain[...].astype(F32)
-    for i in range(32):
-        part[pl.ds(i * 64 + 3, 16, stride=4), :] = gains
 
     def chunk(step, carry):
         volt_copy(step).wait()
@@ -185,20 +160,47 @@
         gathered[pl.ds(t, 16, stride=16), :] = value[:, t * 128 : t * 128 + 128]
     total = gathered[...].T
 
-    copies = []
+    rest = jnp.zeros((64, 64), F32)
     for b in range(8):
-        lanes = [
-            total[0:64, b * 32 : b * 32 + 32],
-            total[64:128, b * 32 : b * 32 + 32],
-            jnp.broadcast_to(row[:, 0:64], (64, 64)),
-        ]
-        rows = pl.ds(b * 256, 256)
-        part[pl.ds(b * 256, 64, stride=4), :] = jnp.concatenate(lanes, axis=1)
-        ready[rows, :] = part[rows, :].astype(BF)
-        copies.append(pltpu.make_async_copy(ready.at[rows, :], out_ref.at[rows, :], sems.at[0, b]))
-        copies[-1].start()
-    for copy in copies:
-        copy.wait()
+        lanes = [total[0:64, b * 32 : b * 32 + 32], total[64:128, b * 32 : b * 32 + 32], rest]
+        rows = jnp.concatenate(lanes, axis=1).astype(BF)
+        for n, k in enumerate((0, 2, 1, 3)):
+            out_ref[b * 64 + n * 16 : b * 64 + n * 16 + 16, :] = rows[k * 16 : k * 16 + 16]
+
+
+def station_part(n):
+    return (lax.shift_right_logical(n, 1) & 7) * 4 + lax.shift_right_logical(n, 8) * 2 + (n & 1)
+
+
+def station_block(n):
+    return lax.shift_right_logical(n, 4) & 15
+
+
+def flag_kernel(index_ref, flag_ref, out_ref):
+    half, block = index_ref[0], index_ref[1]
+    source = iota((16, SPB), 0)
+    wanted = lax.shift_right_logical(source, 1) * 4 + half * 2 + (source & 1)
+    rows = jnp.where(iota((16, SPB), 1) == wanted, 1.0, 0.0).astype(BF)
+    flags = dot(rows, flag_ref[...].astype(F32).astype(BF)).astype(BF)
+    place = (iota((1, 384), 1) + 256 * half + 64 * (block // 4)) & (STATIONS - 1)
+    wanted = station_block(place) * SPB + station_part(place)
+    pick = jnp.where(iota((STATIONS, 384), 0) == wanted, 1.0, 0.0).astype(BF)
+    out_ref[...] = dot(flags, pick)
+
+
+def forward_kernel(recv_ref, flag_ref, gain_ref, out_ref, part):
+    low = iota((32, 128), 1) < 64
+    gains = gain_ref[...].astype(F32)
+    for n in range(16):
+        flags = flag_ref[n : n + 1, :]
+        spectra = recv_ref[n * 32 : n * 32 + 32, :].astype(F32)
+        start = jnp.concatenate([flags[:, 0:64], flags[:, 0:64]], axis=1)
+        part[pl.ds(n * 4, 32, stride=64), :] = jnp.where(low, spectra, jnp.broadcast_to(start, (32, 128)))
+        part[pl.ds(n * 4 + 1, 32, stride=64), :] = jnp.broadcast_to(flags[:, 64:192], (32, 128))
+        part[pl.ds(n * 4 + 2, 32, stride=64), :] = jnp.broadcast_to(flags[:, 192:320], (32, 128))
+        part[pl.ds(n * 4 + 3, 16, stride=64), :] = gains
+        part[pl.ds(n * 4 + 1027, 16, stride=64), :] = gains
+    out_ref[...] = part[...].astype(BF)
 
 
 def steer_kernel(cos_ref, sin_ref, weight_ref, near_e, steer_ref, turned_ref):
@@ -221,7 +223,7 @@
 ):
     part[...] = recv_ref[...].astype(F32)
     first = part[pl.ds(0, 512, stride=4), :]
-    index = index_ref[0]
+    half = index_ref[0]
 
     sent = jnp.concatenate(
         [
@@ -251,11 +253,11 @@
         near_x[p, 1] = jnp.concatenate([own[16:32], -own[0:16]], axis=0).astype(BF)
         far_x[p] = first[:, p * 32 : p * 32 + 32].astype(BF)
 
-    gains = part[pl.ds(index * 64 + 3, 16, stride=4), :].astype(BF)
-    to_row = jnp.where((iota((512, 16), 0) & 15) == iota((512, 16), 1), 1.0, 0.0).astype(BF)
+    gains = part[pl.ds(half * 1024 + 3, 16, stride=64), :].astype(BF)
+    to_row = jnp.where(station_block(iota((512, 16), 0)) == iota((512, 16), 1), 1.0, 0.0).astype(BF)
     spread = dot(to_row, gains)
     lane = iota((512, 128), 1)
-    own_lane = lax.shift_right_logical(lane & 63, 1) == lax.shift_right_logical(iota((512, 128), 0), 4)
+    own_lane = lax.shift_right_logical(lane & 63, 1) == station_part(iota((512, 128), 0))
     spread = jnp.where(own_lane, spread, 0.0).astype(BF)
     source = iota((128, 256), 0)
     target = iota((128, 256), 1)
@@ -310,8 +312,8 @@
             own = near_gain[part_id * 2 + p : part_id * 2 + p + 1]
             steps.append((moment - own * weight_sum) / (1.0 + weight_sum))
 
-    mine = (iota((16, 512), 1) & 15) == iota((16, 512), 0)
-    source = iota((512, 128), 0)
+    mine = station_block(iota((16, 512), 1)) == iota((16, 512), 0)
+    source = station_part(iota((512, 128), 0)) * 2
     target = iota((512, 128), 1)
     placed = jnp.zeros((48, 128), F32)
     for n, value in enumerate(steps):
@@ -320,7 +322,7 @@
         rest = value - hi.astype(F32)
         mid = rest.astype(BF)
         low = (rest - mid.astype(F32)).astype(BF)
-        column = (n // 2) * 64 + lax.shift_right_logical(source, 4) * 2 + (n % 2)
+        column = (n // 2) * 64 + source + (n % 2)
         move = jnp.where(target == column, 1.0, 0.0).astype(BF)
         placed = placed + dot(jnp.concatenate([hi, mid, low], axis=0), move)
     out_ref[...] = placed[0:16] + (placed[16:32] + placed[32:48])
@@ -334,35 +336,54 @@
     return pl.BlockSpec(memory_space=pltpu.HBM)
 
 
-def make_spectra(index, volts, gains, flags):
+def make_spectra(volts):
     window, first, turn, second = filter_tables()
     return pl.pallas_call(
         spectra_kernel,
-        out_shape=jax.ShapeDtypeStruct((4 * CW, 128), BF),
-        in_specs=[pl.BlockSpec(memory_space=pltpu.SMEM)] + [anywhere()] * 7,
-        out_specs=anywhere(),
+        out_shape=jax.ShapeDtypeStruct((CW, 128), BF),
+        in_specs=[anywhere()] * 5,
+        out_specs=whole(),
         scratch_shapes=[
             pltpu.VMEM((CHUNKS, FRAMES_IN, 16, 128), BF),
             pltpu.VMEM((CHUNKS, TAPS, 16, 128), F32),
             pltpu.VMEM((384, 256), BF),
             pltpu.VMEM((2, 128, 128), F32),
             pltpu.VMEM((32, 256), BF),
-            pltpu.VMEM((BLOCKS, 128), BF),
-            pltpu.VMEM((SPB, STATIONS), jnp.int32),
             pltpu.VMEM((NFRAMES, 128, 128), F32),
-            pltpu.VMEM((256, 128), F32),
-            pltpu.VMEM((4 * CW, 128), F32),
-            pltpu.VMEM((4 * CW, 128), BF),
-            pltpu.SemaphoreType.DMA((2, CHUNKS)),
-            pltpu.SemaphoreType.DMA((5,)),
             pltpu.VMEM((NFRAMES * 128, 256), BF),
             pltpu.VMEM((NFRAMES * 128, 256), F32),
             pltpu.VMEM((256, NFRAMES * 128), BF),
             pltpu.VMEM((256, NFRAMES * 128), BF),
+            pltpu.VMEM((256, 128), F32),
+            pltpu.SemaphoreType.DMA((2, CHUNKS)),
+            pltpu.SemaphoreType.DMA((3,)),
         ],
         compiler_params=pltpu.CompilerParams(vmem_limit_bytes=60 * 2**20),
         name="spectra",
-    )(index, volts, jnp.asarray(window), jnp.asarray(first), jnp.asarray(turn), jnp.asarray(second), gains, flags)
+    )(volts, jnp.asarray(window), jnp.asarray(first), jnp.asarray(turn), jnp.asarray(second))
+
+
+def make_flags(index, flags):
+    return pl.pallas_call(
+        flag_kernel,
+        out_shape=jax.ShapeDtypeStruct((16, 384), F32),
+        in_specs=[pl.BlockSpec(memory_space=pltpu.SMEM), whole()],
+        out_specs=whole(),
+        compiler_params=pltpu.CompilerParams(vmem_limit_bytes=16 * 2**20),
+        name="flags",
+    )(index, flags)
+
+
+def make_forward(recv, flags, gains):
+    return pl.pallas_call(
+        forward_kernel,
+        out_shape=jax.ShapeDtypeStruct((4 * STATIONS, 128), BF),
+        in_specs=[whole()] * 3,
+        out_specs=whole(),
+        scratch_shapes=[pltpu.VMEM((4 * STATIONS, 128), F32)],
+        compiler_params=pltpu.CompilerParams(vmem_limit_bytes=16 * 2**20),
+        name="forward",
+    )(recv, flags, gains)
 
 
 def arrange(voltages):
@@ -406,29 +427,34 @@
 
 
 def steering_phases(positions, directions, channel):
-    order = positions.reshape(BLOCKS, SPB, 2).transpose(2, 1, 0).reshape(2, STATIONS)
+    order = positions.reshape(BLOCKS, 8, 2, 2, 2).transpose(4, 2, 0, 1, 3).reshape(2, STATIONS)
     delays = order[0][None, :] * directions[:, 0][:, None] + order[1][None, :] * directions[:, 1][:, None]
     scaled = 2.0 * math.pi * (1.0 + channel.astype(F32) / F)
     phases = scaled * delays
     return jnp.cos(phases), jnp.sin(phases)
 
 
+def exchange(values, axes):
+    return lax.all_to_all(values, axes, split_axis=0, concat_axis=0, tiled=True)
+
+
 def body(voltages, station_gains, positions, directions, weights, baseline_flags):
-    chan_index = lax.axis_index("chan")
-    stn_index = lax.axis_index("stn")
-    index = jnp.reshape(chan_index, (1,)).astype(jnp.int32)
-    channel = chan_index * BLOCKS + stn_index
-    volts = arrange(voltages)
-    payload = make_spectra(index, volts, station_gains[:, 0, :], baseline_flags)
-    recv = lax.all_to_all(
-        payload.reshape(CW, 4, 128), ("chan", "stn"), split_axis=0, concat_axis=0, tiled=True
-    )
+    half = lax.axis_index("z_hi")
+    stn_index = lax.axis_index(STN)
+    index = jnp.stack([half, stn_index]).astype(jnp.int32)
+    channel = lax.axis_index(CHAN) * BLOCKS + stn_index
+    spectra = make_spectra(arrange(voltages)).reshape(16, 32, 128)
+    halfway = exchange(spectra, ("y", "core")).reshape(CW, 128)
+    flags = make_flags(index, baseline_flags)
+    payload = make_forward(halfway, flags, station_gains[:, 0, :])
+    recv = exchange(payload.reshape(32, 64, 128), ("z_hi",) + STN).reshape(4 * STATIONS, 128)
     cos, sin = steering_phases(positions, directions, channel)
-    steps = make_steps(index, recv.reshape(4 * CW, 128), *make_steering(cos, sin, weights))
-    return lax.all_to_all(steps.reshape(BLOCKS, 1, 128), "stn", split_axis=0, concat_axis=0, tiled=True)
+    steps = make_steps(index, recv, *make_steering(cos, sin, weights))
+    return exchange(steps.reshape(BLOCKS, 1, 128), STN)
 
 
 def solution(mesh):
-    in_specs = (P("stn", "chan", None, None), P("chan", "stn", None), P(), P(), P(), P("stn", None))
-    out_specs = P("chan", "stn", None)
-    return jax.shard_map(body, mesh=mesh, in_specs=in_specs, out_specs=out_specs, check_vma=False)
+    parts = Mesh(mesh.devices.reshape(8, 2, 2, 4, 4), CHAN + STN)
+    in_specs = (P(STN, CHAN, None, None), P(CHAN, STN, None), P(), P(), P(), P(STN, None))
+    out_specs = P(CHAN, STN, None)
+    return jax.shard_map(body, mesh=parts, in_specs=in_specs, out_specs=out_specs, check_vma=False)

time: 65.5 us -> 71 us (1.084)
  waiting for transfers between devices: 19.4 us -> 23.4 us
  Pallas kernels: 9.63 us -> 11.9 us
  blocking collectives: 10.7 us -> 9.75 us
    all_to_all x1 -> x2, waiting for transfers between devices: 19.4 us -> 23.4 us  [exchange(): return lax.all_to_all(values, axes, split_axis=0, concat_axis=0, tiled=True)]
    pallas_call x1 -> x3, Pallas kernels: 5.76 us -> 7.37 us  [the longest x1 4.73 us: make_spectra(): pl.pallas_call(spectra_kernel, out_shape=jax.ShapeDtypeStruct((CW, 128),...]
    all_to_all x1, blocking collectives: 10.7 us -> 9.75 us  [exchange(): return lax.all_to_all(values, axes, split_axis=0, concat_axis=0, tiled=True)]
    all_to_all x1 -> x2, starting transfers between devices: 22.2 us -> 21.6 us  [exchange(): return lax.all_to_all(values, axes, split_axis=0, concat_axis=0, tiled=True)]
    unnamed x8 -> x12, local copies, waits for them, and re-layouts: 2.65 us -> 2.64 us
  transfers between devices with their start and end apart: 1 -> 2, of which waited for: 1 -> 2; matrix products, arithmetic and copies ran while one was open for 1% -> 2% of each run, Pallas kernels for 0% -> 1%
where the time goes in v3:
time: 71 us; the launch traced here: 70.5 us
  waiting for transfers between devices  23.4 us (33%)
  starting transfers between devices  21.6 us (30%)
  Pallas kernels  11.9 us (17%)
  blocking collectives  9.75 us (14%)
  local copies, waits for them, and re-layouts  3.37 us (5%)
    all_to_all x2, waiting for transfers between devices, exchange(): return lax.all_to_all(values, axes, split_axis=0, concat_axis=0, tiled=True)  23.4 us
    all_to_all x2, starting transfers between devices, exchange(): return lax.all_to_all(values, axes, split_axis=0, concat_axis=0, tiled=True)  21.6 us
    all_to_all x1, blocking collectives, exchange(): return lax.all_to_all(values, axes, split_axis=0, concat_axis=0, tiled=True)  9.75 us
    pallas_call x1, Pallas kernels, make_spectra(): pl.pallas_call(spectra_kernel, out_shape=jax.ShapeDtypeStruct((CW, 128),...  4.73 us
    pallas_call x1, Pallas kernels, make_steps(): pl.pallas_call(pair_kernel, out_shape=jax.ShapeDtypeStruct((BLOCKS, 128),...  4.28 us
    unnamed x12, local copies, waits for them, and re-layouts  2.64 us
    pallas_call x1, Pallas kernels, make_forward(): pl.pallas_call(forward_kernel, out_shape=jax.ShapeDtypeStruct((4 * STATIO...  1.84 us
  transfers between devices with their start and end apart: 2, of which 2 were waited for; matrix products, arithmetic and copies ran while one was open for 2% of the time, Pallas kernels for 1%

profile of v3, /device:TPU:1, one launch (start us, length us, event | category | flops | bytes accessed | tf_op | source)
XLA Modules:
  0.0 70.5 jit_solution(597779418199405220)
XLA Ops:
  0.0 4.7 %spectra.1 = bf16[512,128]{1,0:T(8,128)(2,1)} custom-call(bf16[31,128,128]{2,1,0:T(8,128)(2,1)} %bitcast.31, f32[8,16,16,128]{3,2,1,0:T(8,128)} %constant.44.clone.win_ref, bf16[384,256]{1,0:T(8,128)(2,1)} %constant.45.clone.first_ref, f32[2,128,128]{2,1,0:T(8,128)} %constant.46.clone.turn_ref, bf16[32,256]{1,0:T(8,128)(2,1)} %constant.47.clone.second_ref), custom_call_target="tpu_custom_call" | custom-call | tf_op jit(solution)/shard_map/spectra/pallas_call | solution.py:341
  4.7 0.0 copy-start
  4.8 10.3 %all-to-all-start = ((bf16[16,32,128]{2,1,0:T(8,128)(2,1)}), bf16[16,32,128]{2,1,0:T(8,128)(2,1)S(1)}, u32[]{:S(2)}, u32[]{:S(2)}) async-start(bf16[16,32,128]{2,1,0:T(8,128)(2,1)} %bitcast.32), calls=%async_computation | async-start | bytes 262144 | tf_op jit(solution)/shard_map/all_to_all | solution.py:438
  15.1 0.1 pad_add_fusion.index_ref
  15.1 0.8 %flags.1.flag_ref = f32[16,384]{1,0:T(8,128)S(1)} custom-call(s32[2]{0:T(128)S(1)} %pad_add_fusion.index_ref, s32[32,512]{1,0:T(8,128)S(1)} %copy-done), custom_call_target="tpu_custom_call" | custom-call | tf_op jit(solution)/shard_map/flags/pallas_call | solution.py:367
  16.0 8.3 %all-to-all-done = bf16[16,32,128]{2,1,0:T(8,128)(2,1)S(1)} async-done(((bf16[16,32,128]{2,1,0:T(8,128)(2,1)}), bf16[16,32,128]{2,1,0:T(8,128)(2,1)S(1)}, u32[]{:S(2)}, u32[]{:S(2)}) %all-to-all-start) | async-done | bytes 131104 | tf_op jit(solution)/shard_map/all_to_all | solution.py:438
  24.3 0.0 copy-done.1
  24.3 1.8 %forward.1 = bf16[2048,128]{1,0:T(8,128)(2,1)} custom-call(bf16[512,128]{1,0:T(8,128)(2,1)S(1)} %bitcast.27, f32[16,384]{1,0:T(8,128)S(1)} %flags.1.flag_ref, bf16[16,128]{1,0:T(8,128)(2,1)S(1)} %bitcast.29), custom_call_target="tpu_custom_call" | custom-call | tf_op jit(solution)/shard_map/forward/pallas_call | solution.py:378
  26.1 11.3 %all-to-all-start.1 = ((bf16[32,64,128]{2,1,0:T(8,128)(2,1)}), bf16[32,64,128]{2,1,0:T(8,128)(2,1)S(1)}, u32[]{:S(2)}, u32[]{:S(2)}) async-start(bf16[32,64,128]{2,1,0:T(8,128)(2,1)} %bitcast.8), calls=%async_computation.1 | async-start | bytes 1048576 | tf_op jit(solution)/shard_map/all_to_all | solution.py:438
  37.4 0.0 copy-start.3
  37.4 0.7 copy-done.3
  38.1 0.1 copy.22.weight_ref
  38.2 0.6 copy-done.2
  38.8 0.4 reshape.35
  39.3 0.1 mul.57
  39.4 0.1 mul.62
  39.6 0.0 copy-start.4
  39.6 0.7 copy-done.4
  40.3 0.3 fusion
  40.6 0.3 steer.1
  40.8 15.1 %all-to-all-done.1 = bf16[32,64,128]{2,1,0:T(8,128)(2,1)S(1)} async-done(((bf16[32,64,128]{2,1,0:T(8,128)(2,1)}), bf16[32,64,128]{2,1,0:T(8,128)(2,1)S(1)}, u32[]{:S(2)}, u32[]{:S(2)}) %all-to-all-start.1) | async-done | bytes 524320 | tf_op jit(solution)/shard_map/all_to_all | solution.py:438
  55.9 4.3 %pairs.1 = f32[16,128]{1,0:T(8,128)S(1)} custom-call(s32[2]{0:T(128)S(1)} %pad_add_fusion.index_ref, bf16[2048,128]{1,0:T(8,128)(2,1)S(1)} %bitcast.26, bf16[2,2,128,512]{3,2,1,0:T(8,128)(2,1)S(1)} %get-tuple-element.8.near_e, f32[512,128]{1,0:T(8,128)S(1)} %get-tuple-element.9.steer_ref, f32[512,128]{1,0:T(8,128)S(1)} %get-tuple-element.10.turned_ref), custom_call_target="tpu_custom_call" | custom-call | tf_op jit(solution)/shard_map/pairs/pallas_call | solution.py:410
  60.2 9.7 %all_to_all.15 = f32[16,1,128]{2,1,0:T(1,128)S(1)} all-to-all(f32[16,1,128]{2,1,0:T(1,128)S(1)} %bitcast.28), channel_id=1, replica_groups=mesh['y'=8,'z_hi'=2,'core'=2,'x'=4,'z_lo'=4] {'x','z_lo'}, dimensions={0} | all-to-all | bytes 16384 | tf_op jit(solution)/shard_map/all_to_all | solution.py:438
  69.9 0.6 copy.25
  (7 shorter events, 0.0 us)
Async XLA Ops:
  4.7 10.4 %copy-start = (s32[32,512]{1,0:T(8,128)S(1)}, s32[32,512]{1,0:T(8,128)}, u32[]{:S(2)}) copy-start(s32[32,512]{1,0:T(8,128)} %flag_ref.1) | copy-start | bytes 196612
  4.8 19.5 %all-to-all-start = ((bf16[16,32,128]{2,1,0:T(8,128)(2,1)}), bf16[16,32,128]{2,1,0:T(8,128)(2,1)S(1)}, u32[]{:S(2)}, u32[]{:S(2)}) async-start(bf16[16,32,128]{2,1,0:T(8,128)(2,1)} %bitcast.32), calls=%async_computation | async-start | bytes 262144 | tf_op jit(solution)/shard_map/all_to_all | solution.py:438
  15.1 9.1 %copy-start.1 = (bf16[16,1,128]{2,0,1:T(8,128)(2,1)S(1)}, bf16[16,1,128]{2,0,1:T(8,128)(2,1)}, u32[]{:S(2)}) copy-start(bf16[16,1,128]{2,0,1:T(8,128)(2,1)} %param.11) | copy-start | bytes 12292
  26.1 29.8 %all-to-all-start.1 = ((bf16[32,64,128]{2,1,0:T(8,128)(2,1)}), bf16[32,64,128]{2,1,0:T(8,128)(2,1)S(1)}, u32[]{:S(2)}, u32[]{:S(2)}) async-start(bf16[32,64,128]{2,1,0:T(8,128)(2,1)} %bitcast.8), calls=%async_computation.1 | async-start | bytes 1048576 | tf_op jit(solution)/shard_map/all_to_all | solution.py:438
  37.4 0.7 copy-start.3
  38.1 0.7 copy-start.2
  39.6 0.7 copy-start.4

commit v4 on v2

--- a/solution.py
+++ b/solution.py
@@ -94,18 +94,17 @@
     second,
     gain,
     flag,
+    pick,
     fold,
-    gathered,
-    part,
-    ready,
-    sems,
-    late,
     left,
     section,
     high,
     low,
+    gathered,
+    part,
+    sems,
+    late,
 ):
-
     def volt_copy(step):
         rows = pl.ds(pl.multiple_of(step * 16, 16), 16)
         return pltpu.make_async_copy(volt_ref.at[:, rows, :], volts.at[step], sems.at[0, step])
@@ -113,19 +112,13 @@
     def window_copy(step):
         return pltpu.make_async_copy(win_ref.at[step], window.at[step], sems.at[1, step])
 
-    early = [
+    others = [
         pltpu.make_async_copy(source, target, late.at[n])
-        for n, (source, target) in enumerate(((gain_ref, gain), (flag_ref, flag)))
+        for n, (source, target) in enumerate(
+            ((first_ref, first), (turn_ref, turn), (second_ref, second), (gain_ref, gain), (flag_ref, flag))
+        )
     ]
-    others = [
-        pltpu.make_async_copy(source, target, late.at[n + 2])
-        for n, (source, target) in enumerate(((first_ref, first), (turn_ref, turn), (second_ref, second)))
-    ]
-    volt_copy(0).start()
-    window_copy(0).start()
-    for copy in early:
-        copy.start()
-    for step in range(1, CHUNKS):
+    for step in range(CHUNKS):
         volt_copy(step).start()
         window_copy(step).start()
     for copy in others:
@@ -134,16 +127,7 @@
     index = index_ref[0]
     place = (iota((1, 384), 1) + 64 * (index // 4)) & (STATIONS - 1)
     wanted = (place & 15) * SPB + lax.shift_right_logical(place, 4)
-    pick = jnp.where(iota((STATIONS, 384), 0) == wanted, 1.0, 0.0).astype(BF)
-    for copy in early:
-        copy.wait()
-    flags = jnp.broadcast_to(flag[pl.ds(index, 1), :].astype(F32), (8, STATIONS)).astype(BF)
-    row = dot(flags, pick)[0:1]
-    part[pl.ds(1, 512, stride=4), :] = jnp.broadcast_to(row[:, 64:192], (512, 128))
-    part[pl.ds(2, 512, stride=4), :] = jnp.broadcast_to(row[:, 192:320], (512, 128))
-    gains = gain[...].astype(F32)
-    for i in range(32):
-        part[pl.ds(i * 64 + 3, 16, stride=4), :] = gains
+    pick[...] = jnp.where(iota((STATIONS, 384), 0) == wanted, 1.0, 0.0).astype(BF)
 
     def chunk(step, carry):
         volt_copy(step).wait()
@@ -185,23 +169,27 @@
         gathered[pl.ds(t, 16, stride=16), :] = value[:, t * 128 : t * 128 + 128]
     total = gathered[...].T
 
-    copies = []
+    flags = jnp.broadcast_to(flag[pl.ds(index, 1), :].astype(F32), (8, STATIONS)).astype(BF)
+    row = dot(flags, pick[...])[0:1]
+
     for b in range(8):
         lanes = [
             total[0:64, b * 32 : b * 32 + 32],
             total[64:128, b * 32 : b * 32 + 32],
             jnp.broadcast_to(row[:, 0:64], (64, 64)),
         ]
-        rows = pl.ds(b * 256, 256)
         part[pl.ds(b * 256, 64, stride=4), :] = jnp.concatenate(lanes, axis=1)
-        ready[rows, :] = part[rows, :].astype(BF)
-        copies.append(pltpu.make_async_copy(ready.at[rows, :], out_ref.at[rows, :], sems.at[0, b]))
-        copies[-1].start()
-    for copy in copies:
-        copy.wait()
-
-
-def steer_kernel(cos_ref, sin_ref, weight_ref, near_e, steer_ref, turned_ref):
+    part[pl.ds(1, 512, stride=4), :] = jnp.broadcast_to(row[:, 64:192], (512, 128))
+    part[pl.ds(2, 512, stride=4), :] = jnp.broadcast_to(row[:, 192:320], (512, 128))
+    gains = gain[...].astype(F32)
+    for i in range(32):
+        part[pl.ds(i * 64 + 3, 16, stride=4), :] = gains
+    out_ref[...] = part[...].astype(BF)
+
+
+def steer_kernel(
+    cos_ref, sin_ref, weight_ref, near_e, steer_ref, turned_ref, own_ref, row_ref, wide_ref, code_ref, move_ref
+):
     cos, sin = cos_ref[...], sin_ref[...]
     steer, turned = [], []
     for p in range(2):
@@ -214,10 +202,46 @@
         near_e[p, 1] = jnp.concatenate([-im, re, -im, re], axis=0).astype(BF)
     steer_ref[...] = jnp.concatenate(steer, axis=0).T
     turned_ref[...] = jnp.concatenate(turned, axis=0).T
+    station = iota((STATIONS, 128), 0)
+    lane = iota((STATIONS, 128), 1)
+    place, block = lax.shift_right_logical(station, 4), station & 15
+    own_ref[...] = jnp.where(lax.shift_right_logical(lane & 63, 1) == place, 1.0, 0.0)
+    row_ref[...] = jnp.where(block == lane, 1.0, 0.0).astype(BF)
+    source = iota((128, 256), 0)
+    target = iota((128, 256), 1)
+    fits = ((source & 1) == (lax.shift_right_logical(target, 6) & 1)) & (
+        lax.shift_right_logical(source, 6) == lax.shift_right_logical(target, 7)
+    )
+    wide_ref[...] = jnp.where(fits, 1.0, 0.0).astype(BF)
+    code = iota((16, 128), 0)
+    lane = iota((16, 128), 1)
+    fits = ((lane & 1) == (code & 1)) & (lax.shift_right_logical(lane, 6) == lax.shift_right_logical(code, 1))
+    code_ref[...] = jnp.where(fits, 1.0, 0.0).astype(BF)
+    for n in range(4):
+        column = (n // 2) * 64 + place * 2 + (n % 2)
+        move_ref[n] = jnp.where(iota((STATIONS, 128), 1) == column, 1.0, 0.0).astype(BF)
 
 
 def pair_kernel(
-    index_ref, recv_ref, near_e, steer_ref, turned_ref, out_ref, part, near_x, far_x, far_e, usable, acc, *products
+    index_ref,
+    recv_ref,
+    near_e,
+    steer_ref,
+    turned_ref,
+    own_ref,
+    row_ref,
+    wide_ref,
+    code_ref,
+    move_ref,
+    out_ref,
+    part,
+    near_x,
+    far_x,
+    far_e,
+    brought,
+    usable,
+    acc,
+    *products,
 ):
     part[...] = recv_ref[...].astype(F32)
     first = part[pl.ds(0, 512, stride=4), :]
@@ -237,12 +261,24 @@
         for b in range(8):
             d = (b - a) % 8
             pieces.append(sent[a * 64 : a * 64 + 64, d * 64 : d * 64 + 64] if d <= 4 else empty)
-        usable[pl.ds(a * 64, 64), :] = jnp.concatenate(pieces, axis=1)
-    brought = usable[...]
-    rows, cols = iota((512, 512), 0), iota((512, 512), 1)
-    ahead = (lax.shift_right_logical(cols, 6) - lax.shift_right_logical(rows, 6)) & 7
-    both = jnp.where(ahead <= 4, brought, brought.T)
-    usable[...] = jnp.where(rows == cols, 0.0, both)
+        brought[pl.ds(a * 64, 64), :] = jnp.concatenate(pieces, axis=1)
+    turned = brought[...].T
+    low = iota((64, 128), 1) < 64
+    for a in range(8):
+        rows = slice(a * 64, a * 64 + 64)
+        for b in range(0, 8, 2):
+            cols = slice(b * 64, b * 64 + 128)
+            direct, back = brought[rows, cols], turned[rows, cols]
+            known = [(n - a) % 8 <= 4 for n in (b, b + 1)]
+            if known == [True, True]:
+                both = direct
+            elif known == [False, False]:
+                both = back
+            else:
+                both = jnp.where(low == known[0], direct, back)
+            if a // 2 == b // 2:
+                both = jnp.where(iota((64, 128), 0) + (a - b) * 64 == iota((64, 128), 1), 0.0, both)
+            usable[rows, cols] = both
 
     xt = first.T
     for p in range(2):
@@ -252,25 +288,14 @@
         far_x[p] = first[:, p * 32 : p * 32 + 32].astype(BF)
 
     gains = part[pl.ds(index * 64 + 3, 16, stride=4), :].astype(BF)
-    to_row = jnp.where((iota((512, 16), 0) & 15) == iota((512, 16), 1), 1.0, 0.0).astype(BF)
-    spread = dot(to_row, gains)
-    lane = iota((512, 128), 1)
-    own_lane = lax.shift_right_logical(lane & 63, 1) == lax.shift_right_logical(iota((512, 128), 0), 4)
-    spread = jnp.where(own_lane, spread, 0.0).astype(BF)
-    source = iota((128, 256), 0)
-    target = iota((128, 256), 1)
-    fits = ((source & 1) == (lax.shift_right_logical(target, 6) & 1)) & (
-        lax.shift_right_logical(source, 6) == lax.shift_right_logical(target, 7)
-    )
-    wide = dot(spread, jnp.where(fits, 1.0, 0.0).astype(BF))
+    gains = jnp.concatenate([gains, jnp.zeros((112, 128), BF)], axis=0)
+    spread = (dot(row_ref[...], gains) * own_ref[...]).astype(BF)
+    wide = dot(spread, wide_ref[...])
     scaled = wide[:, 0:128] * steer_ref[...] + wide[:, 128:256] * turned_ref[...]
     for q in range(2):
         hi, lo = split2(scaled[:, q * 64 : q * 64 + 64])
         far_e[q] = jnp.concatenate([hi, lo], axis=1)
-    code = iota((8, 128), 0)
-    lane = iota((8, 128), 1)
-    fits = ((lane & 1) == (code & 1)) & (lax.shift_right_logical(lane, 6) == lax.shift_right_logical(code, 1))
-    near_gain = dot_nt(jnp.where(fits, 1.0, 0.0).astype(BF), spread)
+    near_gain = dot_nt(code_ref[...], spread)
 
     blocks = [(p, half, q) for p in range(2) for half in range(2) for q in range(2)]
     sums = {}
@@ -311,8 +336,6 @@
             steps.append((moment - own * weight_sum) / (1.0 + weight_sum))
 
     mine = (iota((16, 512), 1) & 15) == iota((16, 512), 0)
-    source = iota((512, 128), 0)
-    target = iota((512, 128), 1)
     placed = jnp.zeros((48, 128), F32)
     for n, value in enumerate(steps):
         value = jnp.where(mine, jnp.broadcast_to(value, (16, 512)), 0.0)
@@ -320,9 +343,7 @@
         rest = value - hi.astype(F32)
         mid = rest.astype(BF)
         low = (rest - mid.astype(F32)).astype(BF)
-        column = (n // 2) * 64 + lax.shift_right_logical(source, 4) * 2 + (n % 2)
-        move = jnp.where(target == column, 1.0, 0.0).astype(BF)
-        placed = placed + dot(jnp.concatenate([hi, mid, low], axis=0), move)
+        placed = placed + dot(jnp.concatenate([hi, mid, low], axis=0), move_ref[n])
     out_ref[...] = placed[0:16] + (placed[16:32] + placed[32:48])
 
 
@@ -340,7 +361,7 @@
         spectra_kernel,
         out_shape=jax.ShapeDtypeStruct((4 * CW, 128), BF),
         in_specs=[pl.BlockSpec(memory_space=pltpu.SMEM)] + [anywhere()] * 7,
-        out_specs=anywhere(),
+        out_specs=whole(),
         scratch_shapes=[
             pltpu.VMEM((CHUNKS, FRAMES_IN, 16, 128), BF),
             pltpu.VMEM((CHUNKS, TAPS, 16, 128), F32),
@@ -349,16 +370,16 @@
             pltpu.VMEM((32, 256), BF),
             pltpu.VMEM((BLOCKS, 128), BF),
             pltpu.VMEM((SPB, STATIONS), jnp.int32),
+            pltpu.VMEM((STATIONS, 384), BF),
             pltpu.VMEM((NFRAMES, 128, 128), F32),
-            pltpu.VMEM((256, 128), F32),
-            pltpu.VMEM((4 * CW, 128), F32),
-            pltpu.VMEM((4 * CW, 128), BF),
-            pltpu.SemaphoreType.DMA((2, CHUNKS)),
-            pltpu.SemaphoreType.DMA((5,)),
             pltpu.VMEM((NFRAMES * 128, 256), BF),
             pltpu.VMEM((NFRAMES * 128, 256), F32),
             pltpu.VMEM((256, NFRAMES * 128), BF),
             pltpu.VMEM((256, NFRAMES * 128), BF),
+            pltpu.VMEM((256, 128), F32),
+            pltpu.VMEM((4 * CW, 128), F32),
+            pltpu.SemaphoreType.DMA((2, CHUNKS)),
+            pltpu.SemaphoreType.DMA((5,)),
         ],
         compiler_params=pltpu.CompilerParams(vmem_limit_bytes=60 * 2**20),
         name="spectra",
@@ -377,19 +398,24 @@
             jax.ShapeDtypeStruct((2, 2, 128, STATIONS), BF),
             jax.ShapeDtypeStruct((STATIONS, 128), F32),
             jax.ShapeDtypeStruct((STATIONS, 128), F32),
+            jax.ShapeDtypeStruct((STATIONS, 128), F32),
+            jax.ShapeDtypeStruct((STATIONS, 128), BF),
+            jax.ShapeDtypeStruct((128, 256), BF),
+            jax.ShapeDtypeStruct((16, 128), BF),
+            jax.ShapeDtypeStruct((4, STATIONS, 128), BF),
         ),
         in_specs=[whole()] * 3,
-        out_specs=(whole(),) * 3,
+        out_specs=(whole(),) * 8,
         compiler_params=pltpu.CompilerParams(vmem_limit_bytes=16 * 2**20),
         name="steer",
     )(cos, sin, weights)
 
 
-def make_steps(index, recv, near_e, steer, turned):
+def make_steps(index, recv, *prepared):
     return pl.pallas_call(
         pair_kernel,
         out_shape=jax.ShapeDtypeStruct((BLOCKS, 128), F32),
-        in_specs=[pl.BlockSpec(memory_space=pltpu.SMEM)] + [whole()] * 4,
+        in_specs=[pl.BlockSpec(memory_space=pltpu.SMEM)] + [whole()] * 9,
         out_specs=whole(),
         scratch_shapes=[
             pltpu.VMEM((4 * STATIONS, 128), F32),
@@ -397,12 +423,13 @@
             pltpu.VMEM((2, STATIONS, 32), BF),
             pltpu.VMEM((2, STATIONS, 128), BF),
             pltpu.VMEM((STATIONS, STATIONS), F32),
+            pltpu.VMEM((STATIONS, STATIONS), F32),
             pltpu.VMEM((3, 2, 8, STATIONS), F32),
         ]
         + [pltpu.VMEM((STATIONS, 256), F32)] * 8,
         compiler_params=pltpu.CompilerParams(vmem_limit_bytes=24 * 2**20),
         name="pairs",
-    )(index, recv, near_e, steer, turned)
+    )(index, recv, *prepared)
 
 
 def steering_phases(positions, directions, channel):

time: 65.5 us -> 64.6 us (0.986)
    pallas_call x1, Pallas kernels: 5.76 us -> 5.08 us  [make_spectra(): pl.pallas_call(spectra_kernel, out_shape=jax.ShapeDtypeStruct((4 * CW, 12...]
  transfers between devices with their start and end apart: 1 -> 1, of which waited for: 1 -> 1; matrix products, arithmetic and copies ran while one was open for 1% -> 1% of each run, Pallas kernels for 0% -> 1%
where the time goes in v4:
time: 64.6 us; the launch traced here: 64.4 us
  starting transfers between devices  22.2 us (34%)
  waiting for transfers between devices  19.1 us (30%)
  blocking collectives  10.7 us (17%)
  Pallas kernels  9 us (14%)
  local copies, waits for them, and re-layouts  2.97 us (5%)
    all_to_all x1, starting transfers between devices, body(): lax.all_to_all(payload.reshape(CW, 4, 128), ('chan', 'stn'), split_axis=0...  22.2 us
    all_to_all x1, waiting for transfers between devices, body(): lax.all_to_all(payload.reshape(CW, 4, 128), ('chan', 'stn'), split_axis=0...  19.1 us
    all_to_all x1, blocking collectives, body(): lax.all_to_all(steps.reshape(BLOCKS, 1, 128), 'stn', split_axis=0, concat...  10.7 us
    pallas_call x1, Pallas kernels, make_spectra(): pl.pallas_call(spectra_kernel, out_shape=jax.ShapeDtypeStruct((4 * CW, 12...  5.08 us
    pallas_call x1, Pallas kernels, make_steps(): pl.pallas_call(pair_kernel, out_shape=jax.ShapeDtypeStruct((BLOCKS, 128),...  3.44 us
    unnamed x8, local copies, waits for them, and re-layouts  2.65 us
  transfers between devices with their start and end apart: 1, of which 1 were waited for; matrix products, arithmetic and copies ran while one was open for 1% of the time, Pallas kernels for 1%

profile of v4, /device:TPU:1, one launch (start us, length us, event | category | flops | bytes accessed | tf_op | source)
XLA Modules:
  0.0 64.4 jit_solution(3872124052445314786)
XLA Ops:
  0.0 5.1 %spectra.1 = bf16[2048,128]{1,0:T(8,128)(2,1)} custom-call(s32[1]{0:T(128)} %bitcast.index_ref, bf16[31,128,128]{2,1,0:T(8,128)(2,1)} %bitcast.22, f32[8,16,16,128]{3,2,1,0:T(8,128)} %constant.26.clone.win_ref, bf16[384,256]{1,0:T(8,128)(2,1)} %constant.27.clone.first_ref, f32[2,128,128]{2,1,0:T(8,128)} %constant.28.clone.turn_ref, ...), custom_call_target="tpu_custom_call" | custom-call | tf_op jit(solution)/shard_map/spectra/pallas_call | solution.py:360
  5.1 22.2 %all-to-all-start = ((bf16[512,4,128]{2,1,0:T(4,128)(2,1)}), bf16[512,4,128]{2,1,0:T(4,128)(2,1)S(1)}, u32[]{:S(2)}, u32[]{:S(2)}) async-start(bf16[512,4,128]{2,1,0:T(4,128)(2,1)} %bitcast.21), calls=%async_computation | async-start | bytes 1048576 | tf_op jit(solution)/shard_map/all_to_all | solution.py:450
  27.3 0.0 copy-start
  27.3 0.7 %copy-done = f32[512,2]{0,1:T(2,128)S(1)} copy-done((f32[512,2]{0,1:T(2,128)S(1)}, f32[512,2]{0,1:T(2,128)}, u32[]{:S(2)}) %copy-start) | copy-done | bytes 4120
  28.0 0.1 reshape.31
  28.0 0.1 copy.19
  28.1 0.1 mul.45
  28.2 0.0 copy-start.1
  28.2 0.1 mul.50
  28.3 0.6 copy-done.1
  28.9 0.1 copy.20.weight_ref
  29.0 0.0 copy-start.2
  29.0 0.7 %copy-done.2 = f32[32,2]{0,1:T(2,128)S(1)} copy-done((f32[32,2]{0,1:T(2,128)S(1)}, f32[32,2]{0,1:T(2,128)}, u32[]{:S(2)}) %copy-start.2) | copy-done | bytes 280
  29.7 0.3 fusion
  30.0 0.5 steer.1
  30.5 19.1 %all-to-all-done = bf16[512,4,128]{2,1,0:T(4,128)(2,1)S(1)} async-done(((bf16[512,4,128]{2,1,0:T(4,128)(2,1)}), bf16[512,4,128]{2,1,0:T(4,128)(2,1)S(1)}, u32[]{:S(2)}, u32[]{:S(2)}) %all-to-all-start) | async-done | bytes 524320 | tf_op jit(solution)/shard_map/all_to_all | solution.py:450
  49.6 3.4 %pairs.1 = f32[16,128]{1,0:T(8,128)S(1)} custom-call(s32[1]{0:T(128)} %bitcast.index_ref, bf16[2048,128]{1,0:T(8,128)(2,1)S(1)} %bitcast.19, bf16[2,2,128,512]{3,2,1,0:T(8,128)(2,1)S(1)} %get-tuple-element.13.near_e, f32[512,128]{1,0:T(8,128)S(1)} %get-tuple-element.14.steer_ref, f32[512,128]{1,0:T(8,128)S(1)} %get-tuple-element.15.turned_ref, ...), custom_call_target="tpu_custom_call" | custom-call | tf_op jit(solution)/shard_map/pairs/pallas_call | solution.py:415
  53.0 10.7 %all_to_all.10 = f32[16,1,128]{2,1,0:T(1,128)S(1)} all-to-all(f32[16,1,128]{2,1,0:T(1,128)S(1)} %bitcast.20), channel_id=1, replica_groups=mesh['chan'=32,'stn'=16] {'stn'}, dimensions={0} | all-to-all | bytes 16384 | tf_op jit(solution)/shard_map/all_to_all | solution.py:455
  63.8 0.6 copy.23
  (2 shorter events, 0.0 us)
Async XLA Ops:
  5.1 44.5 %all-to-all-start = ((bf16[512,4,128]{2,1,0:T(4,128)(2,1)}), bf16[512,4,128]{2,1,0:T(4,128)(2,1)S(1)}, u32[]{:S(2)}, u32[]{:S(2)}) async-start(bf16[512,4,128]{2,1,0:T(4,128)(2,1)} %bitcast.21), calls=%async_computation | async-start | bytes 1048576 | tf_op jit(solution)/shard_map/all_to_all | solution.py:450
  27.3 0.7 %copy-start = (f32[512,2]{0,1:T(2,128)S(1)}, f32[512,2]{0,1:T(2,128)}, u32[]{:S(2)}) copy-start(f32[512,2]{0,1:T(2,128)} %param.12) | copy-start | bytes 12292
  28.2 0.7 %copy-start.1 = (f32[32,2]{0,1:T(2,128)S(1)}, f32[32,2]{0,1:T(2,128)}, u32[]{:S(2)}) copy-start(f32[32,2]{0,1:T(2,128)} %param.14) | copy-start | bytes 772
  29.0 0.7 %copy-start.2 = (f32[32,2]{0,1:T(2,128)S(1)}, f32[32,2]{0,1:T(2,128)}, u32[]{:S(2)}) copy-start(f32[32,2]{0,1:T(2,128)} %param.13) | copy-start | bytes 772

commit v5 on v4

--- a/solution.py
+++ b/solution.py
@@ -77,6 +77,67 @@
     return lax.broadcasted_iota(jnp.int32, shape, dim)
 
 
+def sine_cosine(x):
+    turns = jnp.floor(x * (2.0 / math.pi) + 0.5)
+    r = x - turns * 1.5703125
+    r = r - turns * 4.837512969970703125e-4
+    r = r - turns * 7.54978995489188216e-8
+    z = r * r
+    sine = ((-1.9515295891e-4 * z + 8.3321608736e-3) * z - 1.6666654611e-1) * z * r + r
+    cosine = ((2.443315711809948e-5 * z - 1.388731625493765e-3) * z + 4.166664568298827e-2) * z * z - 0.5 * z + 1.0
+    quarter = turns.astype(jnp.int32) & 3
+    odd = (quarter & 1) == 1
+    sin = jnp.where(odd, cosine, sine)
+    cos = jnp.where(odd, sine, cosine)
+    sin = jnp.where(quarter >= 2, -sin, sin)
+    cos = jnp.where((quarter == 1) | (quarter == 2), -cos, cos)
+    return sin, cos
+
+
+def prepare_steering(channel, position, columns, near_e, steer_ref, turned_ref):
+    east, north = position[0:1, :], position[1:2, :]
+    delays = columns[0:SOURCES, 0:1] * east + columns[0:SOURCES, 1:2] * north
+    scaled = 2.0 * math.pi * (1.0 + channel.astype(F32) / F)
+    sin, cos = sine_cosine(scaled * delays)
+    parts = []
+    for p in range(2):
+        weight = columns[0:SOURCES, 2 + p : 3 + p]
+        parts += [(cos * weight).astype(BF), (-sin * weight).astype(BF)]
+    source, target = iota((STATIONS, STATIONS), 0), iota((1, STATIONS), 1)
+    wanted = (target & 15) * SPB + lax.shift_right_logical(target, 4)
+    ordered = dot(jnp.concatenate(parts, axis=0), jnp.where(source == wanted, 1.0, 0.0).astype(BF))
+    steer, turned = [], []
+    for p in range(2):
+        re, im = ordered[p * 64 : p * 64 + 32], ordered[p * 64 + 32 : p * 64 + 64]
+        steer += [re, im]
+        turned += [-im, re]
+        near_e[p, 0] = jnp.concatenate([re, im, re, im], axis=0).astype(BF)
+        near_e[p, 1] = jnp.concatenate([-im, re, -im, re], axis=0).astype(BF)
+    steer_ref[...] = jnp.concatenate(steer, axis=0).T
+    turned_ref[...] = jnp.concatenate(turned, axis=0).T
+
+
+def prepare_matrices(own_ref, row_ref, wide_ref, code_ref, move_ref):
+    station = iota((STATIONS, 128), 0)
+    lane = iota((STATIONS, 128), 1)
+    place, block = lax.shift_right_logical(station, 4), station & 15
+    own_ref[...] = jnp.where(lax.shift_right_logical(lane & 63, 1) == place, 1.0, 0.0)
+    row_ref[...] = jnp.where(block == lane, 1.0, 0.0).astype(BF)
+    source = iota((128, 256), 0)
+    target = iota((128, 256), 1)
+    fits = ((source & 1) == (lax.shift_right_logical(target, 6) & 1)) & (
+        lax.shift_right_logical(source, 6) == lax.shift_right_logical(target, 7)
+    )
+    wide_ref[...] = jnp.where(fits, 1.0, 0.0).astype(BF)
+    code = iota((16, 128), 0)
+    lane = iota((16, 128), 1)
+    fits = ((lane & 1) == (code & 1)) & (lax.shift_right_logical(lane, 6) == lax.shift_right_logical(code, 1))
+    code_ref[...] = jnp.where(fits, 1.0, 0.0).astype(BF)
+    for n in range(4):
+        column = (n // 2) * 64 + place * 2 + (n % 2)
+        move_ref[n] = jnp.where(iota((STATIONS, 128), 1) == column, 1.0, 0.0).astype(BF)
+
+
 def spectra_kernel(
     index_ref,
     volt_ref,
@@ -86,7 +147,18 @@
     second_ref,
     gain_ref,
     flag_ref,
+    position_ref,
+    direction_ref,
+    weight_ref,
     out_ref,
+    near_e,
+    steer_ref,
+    turned_ref,
+    own_ref,
+    row_ref,
+    wide_ref,
+    code_ref,
+    move_ref,
     volts,
     window,
     first,
@@ -94,6 +166,10 @@
     second,
     gain,
     flag,
+    position,
+    direction,
+    weight,
+    table,
     pick,
     fold,
     left,
@@ -118,16 +194,27 @@
             ((first_ref, first), (turn_ref, turn), (second_ref, second), (gain_ref, gain), (flag_ref, flag))
         )
     ]
+    small = [
+        pltpu.make_async_copy(position_ref, position, late.at[5]),
+        pltpu.make_async_copy(direction_ref, direction, late.at[6]),
+        pltpu.make_async_copy(weight_ref, weight, late.at[7]),
+    ]
+    table[...] = jnp.zeros((8, 128), F32)
+    for copy in small:
+        copy.start()
     for step in range(CHUNKS):
         volt_copy(step).start()
         window_copy(step).start()
     for copy in others:
         copy.start()
 
-    index = index_ref[0]
+    channel = index_ref[0]
+    index = channel // BLOCKS
     place = (iota((1, 384), 1) + 64 * (index // 4)) & (STATIONS - 1)
     wanted = (place & 15) * SPB + lax.shift_right_logical(place, 4)
     pick[...] = jnp.where(iota((STATIONS, 384), 0) == wanted, 1.0, 0.0).astype(BF)
+
+    prepare_matrices(own_ref, row_ref, wide_ref, code_ref, move_ref)
 
     def chunk(step, carry):
         volt_copy(step).wait()
@@ -140,6 +227,11 @@
         return carry
 
     lax.fori_loop(0, CHUNKS, chunk, 0)
+    for copy in small:
+        copy.wait()
+    table[0:2, 0:SOURCES] = direction[...]
+    table[2:4, 0:SOURCES] = weight[...]
+    prepare_steering(channel, position[...], table[...].T, near_e, steer_ref, turned_ref)
     for copy in others:
         copy.wait()
 
@@ -187,41 +279,6 @@
     out_ref[...] = part[...].astype(BF)
 
 
-def steer_kernel(
-    cos_ref, sin_ref, weight_ref, near_e, steer_ref, turned_ref, own_ref, row_ref, wide_ref, code_ref, move_ref
-):
-    cos, sin = cos_ref[...], sin_ref[...]
-    steer, turned = [], []
-    for p in range(2):
-        weight = weight_ref[:, p : p + 1]
-        re = (cos * weight).astype(BF).astype(F32)
-        im = (-sin * weight).astype(BF).astype(F32)
-        steer += [re, im]
-        turned += [-im, re]
-        near_e[p, 0] = jnp.concatenate([re, im, re, im], axis=0).astype(BF)
-        near_e[p, 1] = jnp.concatenate([-im, re, -im, re], axis=0).astype(BF)
-    steer_ref[...] = jnp.concatenate(steer, axis=0).T
-    turned_ref[...] = jnp.concatenate(turned, axis=0).T
-    station = iota((STATIONS, 128), 0)
-    lane = iota((STATIONS, 128), 1)
-    place, block = lax.shift_right_logical(station, 4), station & 15
-    own_ref[...] = jnp.where(lax.shift_right_logical(lane & 63, 1) == place, 1.0, 0.0)
-    row_ref[...] = jnp.where(block == lane, 1.0, 0.0).astype(BF)
-    source = iota((128, 256), 0)
-    target = iota((128, 256), 1)
-    fits = ((source & 1) == (lax.shift_right_logical(target, 6) & 1)) & (
-        lax.shift_right_logical(source, 6) == lax.shift_right_logical(target, 7)
-    )
-    wide_ref[...] = jnp.where(fits, 1.0, 0.0).astype(BF)
-    code = iota((16, 128), 0)
-    lane = iota((16, 128), 1)
-    fits = ((lane & 1) == (code & 1)) & (lax.shift_right_logical(lane, 6) == lax.shift_right_logical(code, 1))
-    code_ref[...] = jnp.where(fits, 1.0, 0.0).astype(BF)
-    for n in range(4):
-        column = (n // 2) * 64 + place * 2 + (n % 2)
-        move_ref[n] = jnp.where(iota((STATIONS, 128), 1) == column, 1.0, 0.0).astype(BF)
-
-
 def pair_kernel(
     index_ref,
     recv_ref,
@@ -245,7 +302,7 @@
 ):
     part[...] = recv_ref[...].astype(F32)
     first = part[pl.ds(0, 512, stride=4), :]
-    index = index_ref[0]
+    index = index_ref[0] // BLOCKS
 
     sent = jnp.concatenate(
         [
@@ -351,17 +408,33 @@
     return pl.BlockSpec(memory_space=pltpu.VMEM)
 
 
+def held(x):
+    return pltpu.with_memory_space_constraint(x, pltpu.HBM)
+
+
 def anywhere():
     return pl.BlockSpec(memory_space=pltpu.HBM)
 
 
-def make_spectra(index, volts, gains, flags):
+def make_spectra(channel, volts, gains, flags, positions, directions, weights):
     window, first, turn, second = filter_tables()
+    operands = [volts, jnp.asarray(window), jnp.asarray(first), jnp.asarray(turn), jnp.asarray(second), gains, flags]
+    operands = [held(x) for x in operands + [positions.T, directions.T, weights.T]]
     return pl.pallas_call(
         spectra_kernel,
-        out_shape=jax.ShapeDtypeStruct((4 * CW, 128), BF),
-        in_specs=[pl.BlockSpec(memory_space=pltpu.SMEM)] + [anywhere()] * 7,
-        out_specs=whole(),
+        out_shape=(
+            pltpu.VMEM((4 * CW, 128), BF),
+            pltpu.VMEM((2, 2, 128, STATIONS), BF),
+            pltpu.VMEM((STATIONS, 128), F32),
+            pltpu.VMEM((STATIONS, 128), F32),
+            pltpu.VMEM((STATIONS, 128), F32),
+            pltpu.VMEM((STATIONS, 128), BF),
+            pltpu.VMEM((128, 256), BF),
+            pltpu.VMEM((16, 128), BF),
+            pltpu.VMEM((4, STATIONS, 128), BF),
+        ),
+        in_specs=[pl.BlockSpec(memory_space=pltpu.SMEM)] + [anywhere()] * 10,
+        out_specs=(whole(),) * 9,
         scratch_shapes=[
             pltpu.VMEM((CHUNKS, FRAMES_IN, 16, 128), BF),
             pltpu.VMEM((CHUNKS, TAPS, 16, 128), F32),
@@ -370,6 +443,10 @@
             pltpu.VMEM((32, 256), BF),
             pltpu.VMEM((BLOCKS, 128), BF),
             pltpu.VMEM((SPB, STATIONS), jnp.int32),
+            pltpu.VMEM((2, STATIONS), F32),
+            pltpu.VMEM((2, SOURCES), F32),
+            pltpu.VMEM((2, SOURCES), F32),
+            pltpu.VMEM((8, 128), F32),
             pltpu.VMEM((STATIONS, 384), BF),
             pltpu.VMEM((NFRAMES, 128, 128), F32),
             pltpu.VMEM((NFRAMES * 128, 256), BF),
@@ -379,36 +456,16 @@
             pltpu.VMEM((256, 128), F32),
             pltpu.VMEM((4 * CW, 128), F32),
             pltpu.SemaphoreType.DMA((2, CHUNKS)),
-            pltpu.SemaphoreType.DMA((5,)),
+            pltpu.SemaphoreType.DMA((8,)),
         ],
-        compiler_params=pltpu.CompilerParams(vmem_limit_bytes=60 * 2**20),
+        compiler_params=pltpu.CompilerParams(vmem_limit_bytes=28 * 2**20),
         name="spectra",
-    )(index, volts, jnp.asarray(window), jnp.asarray(first), jnp.asarray(turn), jnp.asarray(second), gains, flags)
+    )(channel, *operands)
 
 
 def arrange(voltages):
     rows = voltages.reshape(2, FRAMES_IN * 64, 128).transpose(1, 0, 2)
     return rows.reshape(FRAMES_IN, 128, 128)
-
-
-def make_steering(cos, sin, weights):
-    return pl.pallas_call(
-        steer_kernel,
-        out_shape=(
-            jax.ShapeDtypeStruct((2, 2, 128, STATIONS), BF),
-            jax.ShapeDtypeStruct((STATIONS, 128), F32),
-            jax.ShapeDtypeStruct((STATIONS, 128), F32),
-            jax.ShapeDtypeStruct((STATIONS, 128), F32),
-            jax.ShapeDtypeStruct((STATIONS, 128), BF),
-            jax.ShapeDtypeStruct((128, 256), BF),
-            jax.ShapeDtypeStruct((16, 128), BF),
-            jax.ShapeDtypeStruct((4, STATIONS, 128), BF),
-        ),
-        in_specs=[whole()] * 3,
-        out_specs=(whole(),) * 8,
-        compiler_params=pltpu.CompilerParams(vmem_limit_bytes=16 * 2**20),
-        name="steer",
-    )(cos, sin, weights)
 
 
 def make_steps(index, recv, *prepared):
@@ -432,26 +489,15 @@
     )(index, recv, *prepared)
 
 
-def steering_phases(positions, directions, channel):
-    order = positions.reshape(BLOCKS, SPB, 2).transpose(2, 1, 0).reshape(2, STATIONS)
-    delays = order[0][None, :] * directions[:, 0][:, None] + order[1][None, :] * directions[:, 1][:, None]
-    scaled = 2.0 * math.pi * (1.0 + channel.astype(F32) / F)
-    phases = scaled * delays
-    return jnp.cos(phases), jnp.sin(phases)
-
-
 def body(voltages, station_gains, positions, directions, weights, baseline_flags):
-    chan_index = lax.axis_index("chan")
-    stn_index = lax.axis_index("stn")
-    index = jnp.reshape(chan_index, (1,)).astype(jnp.int32)
-    channel = chan_index * BLOCKS + stn_index
-    volts = arrange(voltages)
-    payload = make_spectra(index, volts, station_gains[:, 0, :], baseline_flags)
+    channel = jnp.reshape(lax.axis_index("chan") * BLOCKS + lax.axis_index("stn"), (1,)).astype(jnp.int32)
+    payload, *prepared = make_spectra(
+        channel, arrange(voltages), station_gains[:, 0, :], baseline_flags, positions, directions, weights
+    )
     recv = lax.all_to_all(
         payload.reshape(CW, 4, 128), ("chan", "stn"), split_axis=0, concat_axis=0, tiled=True
     )
-    cos, sin = steering_phases(positions, directions, channel)
-    steps = make_steps(index, recv.reshape(4 * CW, 128), *make_steering(cos, sin, weights))
+    steps = make_steps(channel, recv.reshape(4 * CW, 128), *prepared)
     return lax.all_to_all(steps.reshape(BLOCKS, 1, 128), "stn", split_axis=0, concat_axis=0, tiled=True)
 
 

time: 64.6 us -> 64.3 us (level)
  blocking collectives: 10.7 us -> 55 us
  starting transfers between devices: 22.2 us -> 0 us
  waiting for transfers between devices: 19.1 us -> 0 us
  local copies, waits for them, and re-layouts: 2.97 us -> 0.6 us
    all_to_all x0 -> x1, blocking collectives: none -> 44.3 us  [body(): lax.all_to_all(payload.reshape(CW, 4, 128), ('chan', 'stn'), split_axis=0...]
    all_to_all x1 -> x0, starting transfers between devices: 22.2 us -> none  [body(): lax.all_to_all(payload.reshape(CW, 4, 128), ('chan', 'stn'), split_axis=0...]
    all_to_all x1 -> x0, waiting for transfers between devices: 19.1 us -> none  [body(): lax.all_to_all(payload.reshape(CW, 4, 128), ('chan', 'stn'), split_axis=0...]
    unnamed x8 -> x1, local copies, waits for them, and re-layouts: 2.65 us -> 0.6 us
    pallas_call x2 -> x1, Pallas kernels: 5.56 us -> 4.94 us  [make_spectra(): pl.pallas_call(spectra_kernel, out_shape=(pltpu.VMEM((4 * CW, 128), BF),...]
  transfers between devices with their start and end apart: 1 -> 0, of which waited for: 1 -> 0; matrix products, arithmetic and copies ran while one was open for 1% -> 0% of each run, Pallas kernels for 1% -> 0%
where the time goes in v5:
time: 64.3 us; the launch traced here: 64.2 us
  blocking collectives  55 us (86%)
  Pallas kernels  8.49 us (13%)
    all_to_all x1, blocking collectives, body(): lax.all_to_all(payload.reshape(CW, 4, 128), ('chan', 'stn'), split_axis=0...  44.3 us
    all_to_all x1, blocking collectives, body(): lax.all_to_all(steps.reshape(BLOCKS, 1, 128), 'stn', split_axis=0, concat...  10.7 us
    pallas_call x1, Pallas kernels, make_spectra(): pl.pallas_call(spectra_kernel, out_shape=(pltpu.VMEM((4 * CW, 128), BF),...  4.94 us
    pallas_call x1, Pallas kernels, make_steps(): pl.pallas_call(pair_kernel, out_shape=jax.ShapeDtypeStruct((BLOCKS, 128),...  3.55 us

profile of v5, /device:TPU:1, one launch (start us, length us, event | category | flops | bytes accessed | tf_op | source)
XLA Modules:
  0.0 64.2 jit_solution(16940242069094444801)
XLA Ops:
  0.0 4.9 %spectra.1 = (bf16[2048,128]{1,0:T(8,128)(2,1)S(1)}, bf16[2,2,128,512]{3,2,1,0:T(8,128)(2,1)S(1)}, f32[512,128]{1,0:T(8,128)S(1)}, f32[512,128]{1,0:T(8,128)S(1)...) custom-call(s32[1]{0:T(128)} %bitcast.index_ref, ...), custom_call_target="tpu_custom_call" | custom-call | tf_op jit(solution)/shard_map/spectra/pallas_call | solution.py:423
  4.9 44.3 %all_to_all.10 = bf16[512,4,128]{2,1,0:T(4,128)(2,1)S(1)} all-to-all(bf16[512,4,128]{2,1,0:T(4,128)(2,1)S(1)} %bitcast.16), channel_id=1, replica_groups=mesh['chan'=32,'stn'=16] {'chan','stn'}, dimensions={0} | all-to-all | bytes 1048576 | tf_op jit(solution)/shard_map/all_to_all | solution.py:497
  49.3 3.6 %pairs.1 = f32[16,128]{1,0:T(8,128)S(1)} custom-call(s32[1]{0:T(128)} %bitcast.index_ref, bf16[2048,128]{1,0:T(8,128)(2,1)S(1)} %bitcast.15, bf16[2,2,128,512]{3,2,1,0:T(8,128)(2,1)S(1)} %get-tuple-element.15.near_e, f32[512,128]{1,0:T(8,128)S(1)} %get-tuple-element.16.steer_ref, f32[512,128]{1,0:T(8,128)S(1)} %get-tuple-element.17.turned_ref, ...), custom_call_target="tpu_custom_call" | custom-call | tf_op jit(solution)/shard_map/pairs/pallas_call | solution.py:472
  52.8 10.7 %all_to_all.11 = f32[16,1,128]{2,1,0:T(1,128)S(1)} all-to-all(f32[16,1,128]{2,1,0:T(1,128)S(1)} %bitcast.17), channel_id=1, replica_groups=mesh['chan'=32,'stn'=16] {'stn'}, dimensions={0} | all-to-all | bytes 16384 | tf_op jit(solution)/shard_map/all_to_all | solution.py:501
  63.6 0.6 copy.16

commit v6 on v5

--- a/solution.py
+++ b/solution.py
@@ -6,6 +6,7 @@
 from jax import lax
 from jax.experimental import pallas as pl
 from jax.experimental.pallas import tpu as pltpu
+from jax.sharding import Mesh
 from jax.sharding import PartitionSpec as P
 
 F = 4096
@@ -21,6 +22,9 @@
 CHUNKS = 8
 CHUNK = 16
 ROWS = 256
+CHAN = ("y", "z_hi", "core")
+STN = ("x", "z_lo")
+ORDER = ("core", "y", "z_hi") + STN
 BF = jnp.bfloat16
 F32 = jnp.float32
 
@@ -77,6 +81,15 @@
     return lax.broadcasted_iota(jnp.int32, shape, dim)
 
 
+def place_of(n):
+    return (lax.shift_right_logical(n, 5) & 7) * 4 + (lax.shift_right_logical(n, 4) & 1) * 2 + lax.shift_right_logical(n, 8)
+
+
+def number_of(channel):
+    group = channel // BLOCKS
+    return (group % 2) * 256 + (group // 4) * 32 + ((group // 2) % 2) * 16 + channel % BLOCKS
+
+
 def sine_cosine(x):
     turns = jnp.floor(x * (2.0 / math.pi) + 0.5)
     r = x - turns * 1.5703125
@@ -104,7 +117,7 @@
         weight = columns[0:SOURCES, 2 + p : 3 + p]
         parts += [(cos * weight).astype(BF), (-sin * weight).astype(BF)]
     source, target = iota((STATIONS, STATIONS), 0), iota((1, STATIONS), 1)
-    wanted = (target & 15) * SPB + lax.shift_right_logical(target, 4)
+    wanted = (target & 15) * SPB + place_of(target)
     ordered = dot(jnp.concatenate(parts, axis=0), jnp.where(source == wanted, 1.0, 0.0).astype(BF))
     steer, turned = [], []
     for p in range(2):
@@ -120,7 +133,7 @@
 def prepare_matrices(own_ref, row_ref, wide_ref, code_ref, move_ref):
     station = iota((STATIONS, 128), 0)
     lane = iota((STATIONS, 128), 1)
-    place, block = lax.shift_right_logical(station, 4), station & 15
+    place, block = place_of(station), station & 15
     own_ref[...] = jnp.where(lax.shift_right_logical(lane & 63, 1) == place, 1.0, 0.0)
     row_ref[...] = jnp.where(block == lane, 1.0, 0.0).astype(BF)
     source = iota((128, 256), 0)
@@ -210,8 +223,8 @@
 
     channel = index_ref[0]
     index = channel // BLOCKS
-    place = (iota((1, 384), 1) + 64 * (index // 4)) & (STATIONS - 1)
-    wanted = (place & 15) * SPB + lax.shift_right_logical(place, 4)
+    place = (iota((1, 384), 1) + 64 * (number_of(channel) // 64)) & (STATIONS - 1)
+    wanted = (place & 15) * SPB + place_of(place)
     pick[...] = jnp.where(iota((STATIONS, 384), 0) == wanted, 1.0, 0.0).astype(BF)
 
     prepare_matrices(own_ref, row_ref, wide_ref, code_ref, move_ref)
@@ -270,7 +283,10 @@
             total[64:128, b * 32 : b * 32 + 32],
             jnp.broadcast_to(row[:, 0:64], (64, 64)),
         ]
-        part[pl.ds(b * 256, 64, stride=4), :] = jnp.concatenate(lanes, axis=1)
+        rows = jnp.concatenate(lanes, axis=1)
+        for n in range(4):
+            target = (n % 2) * 256 + b * 32 + (n // 2) * 16
+            part[pl.ds(target * 4, 16, stride=4), :] = rows[n * 16 : n * 16 + 16]
     part[pl.ds(1, 512, stride=4), :] = jnp.broadcast_to(row[:, 64:192], (512, 128))
     part[pl.ds(2, 512, stride=4), :] = jnp.broadcast_to(row[:, 192:320], (512, 128))
     gains = gain[...].astype(F32)
@@ -302,7 +318,7 @@
 ):
     part[...] = recv_ref[...].astype(F32)
     first = part[pl.ds(0, 512, stride=4), :]
-    index = index_ref[0] // BLOCKS
+    channel = index_ref[0]
 
     sent = jnp.concatenate(
         [
@@ -344,7 +360,7 @@
         near_x[p, 1] = jnp.concatenate([own[16:32], -own[0:16]], axis=0).astype(BF)
         far_x[p] = first[:, p * 32 : p * 32 + 32].astype(BF)
 
-    gains = part[pl.ds(index * 64 + 3, 16, stride=4), :].astype(BF)
+    gains = part[pl.ds((number_of(channel) - channel % BLOCKS) * 4 + 3, 16, stride=4), :].astype(BF)
     gains = jnp.concatenate([gains, jnp.zeros((112, 128), BF)], axis=0)
     spread = (dot(row_ref[...], gains) * own_ref[...]).astype(BF)
     wide = dot(spread, wide_ref[...])
@@ -489,19 +505,22 @@
     )(index, recv, *prepared)
 
 
+def exchange(values, axes):
+    return lax.all_to_all(values, axes, split_axis=0, concat_axis=0, tiled=True)
+
+
 def body(voltages, station_gains, positions, directions, weights, baseline_flags):
-    channel = jnp.reshape(lax.axis_index("chan") * BLOCKS + lax.axis_index("stn"), (1,)).astype(jnp.int32)
+    channel = jnp.reshape(lax.axis_index(CHAN) * BLOCKS + lax.axis_index(STN), (1,)).astype(jnp.int32)
     payload, *prepared = make_spectra(
         channel, arrange(voltages), station_gains[:, 0, :], baseline_flags, positions, directions, weights
     )
-    recv = lax.all_to_all(
-        payload.reshape(CW, 4, 128), ("chan", "stn"), split_axis=0, concat_axis=0, tiled=True
-    )
+    recv = exchange(payload.reshape(CW, 4, 128), ORDER)
     steps = make_steps(channel, recv.reshape(4 * CW, 128), *prepared)
-    return lax.all_to_all(steps.reshape(BLOCKS, 1, 128), "stn", split_axis=0, concat_axis=0, tiled=True)
+    return exchange(steps.reshape(BLOCKS, 1, 128), STN)
 
 
 def solution(mesh):
-    in_specs = (P("stn", "chan", None, None), P("chan", "stn", None), P(), P(), P(), P("stn", None))
-    out_specs = P("chan", "stn", None)
-    return jax.shard_map(body, mesh=mesh, in_specs=in_specs, out_specs=out_specs, check_vma=False)
+    parts = Mesh(mesh.devices.reshape(8, 2, 2, 4, 4), CHAN + STN)
+    in_specs = (P(STN, CHAN, None, None), P(CHAN, STN, None), P(), P(), P(), P(STN, None))
+    out_specs = P(CHAN, STN, None)
+    return jax.shard_map(body, mesh=parts, in_specs=in_specs, out_specs=out_specs, check_vma=False)

time: 64.3 us -> 63.9 us (level)
  blocking collectives: 55 us -> 54.3 us
    all_to_all x2, blocking collectives: 55 us -> 54.3 us  [exchange(): return lax.all_to_all(values, axes, split_axis=0, concat_axis=0, tiled=True)]
where the time goes in v6:
time: 63.9 us; the launch traced here: 63.4 us
  blocking collectives  54.3 us (85%)
  Pallas kernels  8.48 us (13%)
    all_to_all x2, blocking collectives, exchange(): return lax.all_to_all(values, axes, split_axis=0, concat_axis=0, tiled=True)  54.3 us
    pallas_call x1, Pallas kernels, make_spectra(): pl.pallas_call(spectra_kernel, out_shape=(pltpu.VMEM((4 * CW, 128), BF),...  4.93 us
    pallas_call x1, Pallas kernels, make_steps(): pl.pallas_call(pair_kernel, out_shape=jax.ShapeDtypeStruct((BLOCKS, 128),...  3.55 us

profile of v6, /device:TPU:1, one launch (start us, length us, event | category | flops | bytes accessed | tf_op | source)
XLA Modules:
  0.0 63.4 jit_solution(5463124695207019579)
XLA Ops:
  0.0 4.9 %spectra.1 = (bf16[2048,128]{1,0:T(8,128)(2,1)S(1)}, bf16[2,2,128,512]{3,2,1,0:T(8,128)(2,1)S(1)}, f32[512,128]{1,0:T(8,128)S(1)}, f32[512,128]{1,0:T(8,128)S(1)...) custom-call(s32[1]{0:T(128)} %bitcast.index_ref, ...), custom_call_target="tpu_custom_call" | custom-call | tf_op jit(solution)/shard_map/spectra/pallas_call | solution.py:439
  4.9 44.8 %all_to_all.10 = bf16[512,4,128]{2,1,0:T(4,128)(2,1)S(1)} all-to-all(bf16[512,4,128]{2,1,0:T(4,128)(2,1)S(1)} %bitcast.16), channel_id=1, replica_groups=mesh['y'=8,'z_hi'=2,'core'=2,'x'=4,'z_lo'=4] {'core','y','z_hi','x','z_lo'}, dimensions={0} | all-to-all | bytes 1048576 | tf_op jit(solution)/shard_map/all_to_all | solution.py:509
  49.7 3.5 %pairs.1 = f32[16,128]{1,0:T(8,128)S(1)} custom-call(s32[1]{0:T(128)} %bitcast.index_ref, bf16[2048,128]{1,0:T(8,128)(2,1)S(1)} %bitcast.15, bf16[2,2,128,512]{3,2,1,0:T(8,128)(2,1)S(1)} %get-tuple-element.15.near_e, f32[512,128]{1,0:T(8,128)S(1)} %get-tuple-element.16.steer_ref, f32[512,128]{1,0:T(8,128)S(1)} %get-tuple-element.17.turned_ref, ...), custom_call_target="tpu_custom_call" | custom-call | tf_op jit(solution)/shard_map/pairs/pallas_call | solution.py:488
  53.3 9.5 %all_to_all.11 = f32[16,1,128]{2,1,0:T(1,128)S(1)} all-to-all(f32[16,1,128]{2,1,0:T(1,128)S(1)} %bitcast.17), channel_id=1, replica_groups=mesh['y'=8,'z_hi'=2,'core'=2,'x'=4,'z_lo'=4] {'x','z_lo'}, dimensions={0} | all-to-all | bytes 16384 | tf_op jit(solution)/shard_map/all_to_all | solution.py:509
  62.8 0.6 copy.16

commit v7 on v6

--- a/solution.py
+++ b/solution.py
@@ -272,7 +272,7 @@
     value = main[0:16] + (main[16:32] + rest)
     for t in range(NFRAMES):
         gathered[pl.ds(t, 16, stride=16), :] = value[:, t * 128 : t * 128 + 128]
-    total = gathered[...].T
+    total = gathered[0:256].T
 
     flags = jnp.broadcast_to(flag[pl.ds(index, 1), :].astype(F32), (8, STATIONS)).astype(BF)
     row = dot(flags, pick[...])[0:1]
@@ -292,7 +292,7 @@
     gains = gain[...].astype(F32)
     for i in range(32):
         part[pl.ds(i * 64 + 3, 16, stride=4), :] = gains
-    out_ref[...] = part[...].astype(BF)
+    out_ref[...] = part[0 : 4 * CW, :].astype(BF)
 
 
 def pair_kernel(
@@ -316,7 +316,7 @@
     acc,
     *products,
 ):
-    part[...] = recv_ref[...].astype(F32)
+    part[0 : 4 * STATIONS, :] = recv_ref[...].astype(F32)
     first = part[pl.ds(0, 512, stride=4), :]
     channel = index_ref[0]
 
@@ -469,8 +469,8 @@
             pltpu.VMEM((NFRAMES * 128, 256), F32),
             pltpu.VMEM((256, NFRAMES * 128), BF),
             pltpu.VMEM((256, NFRAMES * 128), BF),
-            pltpu.VMEM((256, 128), F32),
-            pltpu.VMEM((4 * CW, 128), F32),
+            pltpu.VMEM((256 + 16, 128), F32),
+            pltpu.VMEM((4 * CW + 64, 128), F32),
             pltpu.SemaphoreType.DMA((2, CHUNKS)),
             pltpu.SemaphoreType.DMA((8,)),
         ],
@@ -491,7 +491,7 @@
         in_specs=[pl.BlockSpec(memory_space=pltpu.SMEM)] + [whole()] * 9,
         out_specs=whole(),
         scratch_shapes=[
-            pltpu.VMEM((4 * STATIONS, 128), F32),
+            pltpu.VMEM((4 * STATIONS + 64, 128), F32),
             pltpu.VMEM((2, 2, 32, STATIONS), BF),
             pltpu.VMEM((2, STATIONS, 32), BF),
             pltpu.VMEM((2, STATIONS, 128), BF),

time: 63.9 us -> 63.9 us (level)
  no operation moved by 1% of the time
where the time goes in v7:
time: 63.9 us; the launch traced here: 63.4 us
  blocking collectives  54.3 us (85%)
  Pallas kernels  8.49 us (13%)
    all_to_all x2, blocking collectives, exchange(): return lax.all_to_all(values, axes, split_axis=0, concat_axis=0, tiled=True)  54.3 us
    pallas_call x1, Pallas kernels, make_spectra(): pl.pallas_call(spectra_kernel, out_shape=(pltpu.VMEM((4 * CW, 128), BF),...  4.94 us
    pallas_call x1, Pallas kernels, make_steps(): pl.pallas_call(pair_kernel, out_shape=jax.ShapeDtypeStruct((BLOCKS, 128),...  3.55 us

profile of v7, /device:TPU:1, one launch (start us, length us, event | category | flops | bytes accessed | tf_op | source)
XLA Modules:
  0.0 63.4 jit_solution(4157510441574828015)
XLA Ops:
  0.0 4.9 %spectra.1 = (bf16[2048,128]{1,0:T(8,128)(2,1)S(1)}, bf16[2,2,128,512]{3,2,1,0:T(8,128)(2,1)S(1)}, f32[512,128]{1,0:T(8,128)S(1)}, f32[512,128]{1,0:T(8,128)S(1)...) custom-call(s32[1]{0:T(128)} %bitcast.index_ref, ...), custom_call_target="tpu_custom_call" | custom-call | tf_op jit(solution)/shard_map/spectra/pallas_call | solution.py:439
  4.9 44.8 %all_to_all.10 = bf16[512,4,128]{2,1,0:T(4,128)(2,1)S(1)} all-to-all(bf16[512,4,128]{2,1,0:T(4,128)(2,1)S(1)} %bitcast.16), channel_id=1, replica_groups=mesh['y'=8,'z_hi'=2,'core'=2,'x'=4,'z_lo'=4] {'core','y','z_hi','x','z_lo'}, dimensions={0} | all-to-all | bytes 1048576 | tf_op jit(solution)/shard_map/all_to_all | solution.py:509
  49.7 3.6 %pairs.1 = f32[16,128]{1,0:T(8,128)S(1)} custom-call(s32[1]{0:T(128)} %bitcast.index_ref, bf16[2048,128]{1,0:T(8,128)(2,1)S(1)} %bitcast.15, bf16[2,2,128,512]{3,2,1,0:T(8,128)(2,1)S(1)} %get-tuple-element.15.near_e, f32[512,128]{1,0:T(8,128)S(1)} %get-tuple-element.16.steer_ref, f32[512,128]{1,0:T(8,128)S(1)} %get-tuple-element.17.turned_ref, ...), custom_call_target="tpu_custom_call" | custom-call | tf_op jit(solution)/shard_map/pairs/pallas_call | solution.py:488
  53.3 9.5 %all_to_all.11 = f32[16,1,128]{2,1,0:T(1,128)S(1)} all-to-all(f32[16,1,128]{2,1,0:T(1,128)S(1)} %bitcast.17), channel_id=1, replica_groups=mesh['y'=8,'z_hi'=2,'core'=2,'x'=4,'z_lo'=4] {'x','z_lo'}, dimensions={0} | all-to-all | bytes 16384 | tf_op jit(solution)/shard_map/all_to_all | solution.py:509
  62.8 0.6 copy.16

commit v8 on v7

--- a/solution.py
+++ b/solution.py
@@ -24,7 +24,7 @@
 ROWS = 256
 CHAN = ("y", "z_hi", "core")
 STN = ("x", "z_lo")
-ORDER = ("core", "y", "z_hi") + STN
+ORDER = ("y", "z_hi") + STN + ("core",)
 BF = jnp.bfloat16
 F32 = jnp.float32
 
@@ -82,12 +82,16 @@
 
 
 def place_of(n):
-    return (lax.shift_right_logical(n, 5) & 7) * 4 + (lax.shift_right_logical(n, 4) & 1) * 2 + lax.shift_right_logical(n, 8)
+    return lax.shift_right_logical(n, 6) * 4 + (lax.shift_right_logical(n, 5) & 1) * 2 + (n & 1)
+
+
+def block_of(n):
+    return lax.shift_right_logical(n, 1) & (BLOCKS - 1)
 
 
 def number_of(channel):
     group = channel // BLOCKS
-    return (group % 2) * 256 + (group // 4) * 32 + ((group // 2) % 2) * 16 + channel % BLOCKS
+    return (group // 2) * 32 + (channel % BLOCKS) * 2 + group % 2
 
 
 def sine_cosine(x):
@@ -117,7 +121,7 @@
         weight = columns[0:SOURCES, 2 + p : 3 + p]
         parts += [(cos * weight).astype(BF), (-sin * weight).astype(BF)]
     source, target = iota((STATIONS, STATIONS), 0), iota((1, STATIONS), 1)
-    wanted = (target & 15) * SPB + place_of(target)
+    wanted = block_of(target) * SPB + place_of(target)
     ordered = dot(jnp.concatenate(parts, axis=0), jnp.where(source == wanted, 1.0, 0.0).astype(BF))
     steer, turned = [], []
     for p in range(2):
@@ -133,7 +137,7 @@
 def prepare_matrices(own_ref, row_ref, wide_ref, code_ref, move_ref):
     station = iota((STATIONS, 128), 0)
     lane = iota((STATIONS, 128), 1)
-    place, block = place_of(station), station & 15
+    place, block = place_of(station), block_of(station)
     own_ref[...] = jnp.where(lax.shift_right_logical(lane & 63, 1) == place, 1.0, 0.0)
     row_ref[...] = jnp.where(block == lane, 1.0, 0.0).astype(BF)
     source = iota((128, 256), 0)
@@ -224,7 +228,7 @@
     channel = index_ref[0]
     index = channel // BLOCKS
     place = (iota((1, 384), 1) + 64 * (number_of(channel) // 64)) & (STATIONS - 1)
-    wanted = (place & 15) * SPB + place_of(place)
+    wanted = block_of(place) * SPB + place_of(place)
     pick[...] = jnp.where(iota((STATIONS, 384), 0) == wanted, 1.0, 0.0).astype(BF)
 
     prepare_matrices(own_ref, row_ref, wide_ref, code_ref, move_ref)
@@ -285,13 +289,13 @@
         ]
         rows = jnp.concatenate(lanes, axis=1)
         for n in range(4):
-            target = (n % 2) * 256 + b * 32 + (n // 2) * 16
-            part[pl.ds(target * 4, 16, stride=4), :] = rows[n * 16 : n * 16 + 16]
+            target = b * 64 + (n // 2) * 32 + n % 2
+            part[pl.ds(target * 4, 16, stride=8), :] = rows[n * 16 : n * 16 + 16]
     part[pl.ds(1, 512, stride=4), :] = jnp.broadcast_to(row[:, 64:192], (512, 128))
     part[pl.ds(2, 512, stride=4), :] = jnp.broadcast_to(row[:, 192:320], (512, 128))
     gains = gain[...].astype(F32)
     for i in range(32):
-        part[pl.ds(i * 64 + 3, 16, stride=4), :] = gains
+        part[pl.ds((i // 2) * 128 + (i % 2) * 4 + 3, 16, stride=8), :] = gains
     out_ref[...] = part[0 : 4 * CW, :].astype(BF)
 
 
@@ -360,7 +364,7 @@
         near_x[p, 1] = jnp.concatenate([own[16:32], -own[0:16]], axis=0).astype(BF)
         far_x[p] = first[:, p * 32 : p * 32 + 32].astype(BF)
 
-    gains = part[pl.ds((number_of(channel) - channel % BLOCKS) * 4 + 3, 16, stride=4), :].astype(BF)
+    gains = part[pl.ds(number_of(channel - channel % BLOCKS) * 4 + 3, 16, stride=8), :].astype(BF)
     gains = jnp.concatenate([gains, jnp.zeros((112, 128), BF)], axis=0)
     spread = (dot(row_ref[...], gains) * own_ref[...]).astype(BF)
     wide = dot(spread, wide_ref[...])
@@ -408,7 +412,7 @@
             own = near_gain[part_id * 2 + p : part_id * 2 + p + 1]
             steps.append((moment - own * weight_sum) / (1.0 + weight_sum))
 
-    mine = (iota((16, 512), 1) & 15) == iota((16, 512), 0)
+    mine = block_of(iota((16, 512), 1)) == iota((16, 512), 0)
     placed = jnp.zeros((48, 128), F32)
     for n, value in enumerate(steps):
         value = jnp.where(mine, jnp.broadcast_to(value, (16, 512)), 0.0)

time: 63.9 us -> 64 us (level)
  no operation moved by 1% of the time
where the time goes in v8:
time: 64 us; the launch traced here: 63.8 us
  blocking collectives  54.7 us (85%)
  Pallas kernels  8.49 us (13%)
    all_to_all x2, blocking collectives, exchange(): return lax.all_to_all(values, axes, split_axis=0, concat_axis=0, tiled=True)  54.7 us
    pallas_call x1, Pallas kernels, make_spectra(): pl.pallas_call(spectra_kernel, out_shape=(pltpu.VMEM((4 * CW, 128), BF),...  4.94 us
    pallas_call x1, Pallas kernels, make_steps(): pl.pallas_call(pair_kernel, out_shape=jax.ShapeDtypeStruct((BLOCKS, 128),...  3.55 us

profile of v8, /device:TPU:1, one launch (start us, length us, event | category | flops | bytes accessed | tf_op | source)
XLA Modules:
  0.0 63.8 jit_solution(12852019358681715260)
XLA Ops:
  0.0 4.9 %spectra.1 = (bf16[2048,128]{1,0:T(8,128)(2,1)S(1)}, bf16[2,2,128,512]{3,2,1,0:T(8,128)(2,1)S(1)}, f32[512,128]{1,0:T(8,128)S(1)}, f32[512,128]{1,0:T(8,128)S(1)...) custom-call(s32[1]{0:T(128)} %bitcast.index_ref, ...), custom_call_target="tpu_custom_call" | custom-call | tf_op jit(solution)/shard_map/spectra/pallas_call | solution.py:443
  4.9 44.7 %all_to_all.10 = bf16[512,4,128]{2,1,0:T(4,128)(2,1)S(1)} all-to-all(bf16[512,4,128]{2,1,0:T(4,128)(2,1)S(1)} %bitcast.16), channel_id=1, replica_groups=mesh['y'=8,'z_hi'=2,'core'=2,'x'=4,'z_lo'=4] {'y','z_hi','x','z_lo','core'}, dimensions={0} | all-to-all | bytes 1048576 | tf_op jit(solution)/shard_map/all_to_all | solution.py:513
  49.7 3.6 %pairs.1 = f32[16,128]{1,0:T(8,128)S(1)} custom-call(s32[1]{0:T(128)} %bitcast.index_ref, bf16[2048,128]{1,0:T(8,128)(2,1)S(1)} %bitcast.15, bf16[2,2,128,512]{3,2,1,0:T(8,128)(2,1)S(1)} %get-tuple-element.15.near_e, f32[512,128]{1,0:T(8,128)S(1)} %get-tuple-element.16.steer_ref, f32[512,128]{1,0:T(8,128)S(1)} %get-tuple-element.17.turned_ref, ...), custom_call_target="tpu_custom_call" | custom-call | tf_op jit(solution)/shard_map/pairs/pallas_call | solution.py:492
  53.2 10.0 %all_to_all.11 = f32[16,1,128]{2,1,0:T(1,128)S(1)} all-to-all(f32[16,1,128]{2,1,0:T(1,128)S(1)} %bitcast.17), channel_id=1, replica_groups=mesh['y'=8,'z_hi'=2,'core'=2,'x'=4,'z_lo'=4] {'x','z_lo'}, dimensions={0} | all-to-all | bytes 16384 | tf_op jit(solution)/shard_map/all_to_all | solution.py:513
  63.2 0.6 copy.16

commit v9 on v5

--- a/solution.py
+++ b/solution.py
@@ -103,12 +103,9 @@
     for p in range(2):
         weight = columns[0:SOURCES, 2 + p : 3 + p]
         parts += [(cos * weight).astype(BF), (-sin * weight).astype(BF)]
-    source, target = iota((STATIONS, STATIONS), 0), iota((1, STATIONS), 1)
-    wanted = (target & 15) * SPB + lax.shift_right_logical(target, 4)
-    ordered = dot(jnp.concatenate(parts, axis=0), jnp.where(source == wanted, 1.0, 0.0).astype(BF))
     steer, turned = [], []
     for p in range(2):
-        re, im = ordered[p * 64 : p * 64 + 32], ordered[p * 64 + 32 : p * 64 + 64]
+        re, im = parts[2 * p].astype(F32), parts[2 * p + 1].astype(F32)
         steer += [re, im]
         turned += [-im, re]
         near_e[p, 0] = jnp.concatenate([re, im, re, im], axis=0).astype(BF)
@@ -120,7 +117,7 @@
 def prepare_matrices(own_ref, row_ref, wide_ref, code_ref, move_ref):
     station = iota((STATIONS, 128), 0)
     lane = iota((STATIONS, 128), 1)
-    place, block = lax.shift_right_logical(station, 4), station & 15
+    place, block = station & (SPB - 1), lax.shift_right_logical(station, 5)
     own_ref[...] = jnp.where(lax.shift_right_logical(lane & 63, 1) == place, 1.0, 0.0)
     row_ref[...] = jnp.where(block == lane, 1.0, 0.0).astype(BF)
     source = iota((128, 256), 0)
@@ -210,9 +207,8 @@
 
     channel = index_ref[0]
     index = channel // BLOCKS
-    place = (iota((1, 384), 1) + 64 * (index // 4)) & (STATIONS - 1)
-    wanted = (place & 15) * SPB + lax.shift_right_logical(place, 4)
-    pick[...] = jnp.where(iota((STATIONS, 384), 0) == wanted, 1.0, 0.0).astype(BF)
+    place = (iota((1, 384), 1) + 64 * ((channel % BLOCKS) // 2)) & (STATIONS - 1)
+    pick[...] = jnp.where(iota((STATIONS, 384), 0) == place, 1.0, 0.0).astype(BF)
 
     prepare_matrices(own_ref, row_ref, wide_ref, code_ref, move_ref)
 
@@ -270,12 +266,14 @@
             total[64:128, b * 32 : b * 32 + 32],
             jnp.broadcast_to(row[:, 0:64], (64, 64)),
         ]
-        part[pl.ds(b * 256, 64, stride=4), :] = jnp.concatenate(lanes, axis=1)
+        rows = jnp.concatenate(lanes, axis=1)
+        for n in range(4):
+            part[pl.ds((4 * b + n) * 4, 16, stride=128), :] = rows[n * 16 : n * 16 + 16]
     part[pl.ds(1, 512, stride=4), :] = jnp.broadcast_to(row[:, 64:192], (512, 128))
     part[pl.ds(2, 512, stride=4), :] = jnp.broadcast_to(row[:, 192:320], (512, 128))
     gains = gain[...].astype(F32)
     for i in range(32):
-        part[pl.ds(i * 64 + 3, 16, stride=4), :] = gains
+        part[pl.ds(i * 4 + 3, 16, stride=128), :] = gains
     out_ref[...] = part[...].astype(BF)
 
 
@@ -344,7 +342,7 @@
         near_x[p, 1] = jnp.concatenate([own[16:32], -own[0:16]], axis=0).astype(BF)
         far_x[p] = first[:, p * 32 : p * 32 + 32].astype(BF)
 
-    gains = part[pl.ds(index * 64 + 3, 16, stride=4), :].astype(BF)
+    gains = part[pl.ds(index * 4 + 3, 16, stride=128), :].astype(BF)
     gains = jnp.concatenate([gains, jnp.zeros((112, 128), BF)], axis=0)
     spread = (dot(row_ref[...], gains) * own_ref[...]).astype(BF)
     wide = dot(spread, wide_ref[...])
@@ -392,7 +390,7 @@
             own = near_gain[part_id * 2 + p : part_id * 2 + p + 1]
             steps.append((moment - own * weight_sum) / (1.0 + weight_sum))
 
-    mine = (iota((16, 512), 1) & 15) == iota((16, 512), 0)
+    mine = lax.shift_right_logical(iota((16, 512), 1), 5) == iota((16, 512), 0)
     placed = jnp.zeros((48, 128), F32)
     for n, value in enumerate(steps):
         value = jnp.where(mine, jnp.broadcast_to(value, (16, 512)), 0.0)
@@ -495,7 +493,7 @@
         channel, arrange(voltages), station_gains[:, 0, :], baseline_flags, positions, directions, weights
     )
     recv = lax.all_to_all(
-        payload.reshape(CW, 4, 128), ("chan", "stn"), split_axis=0, concat_axis=0, tiled=True
+        payload.reshape(CW, 4, 128), ("stn", "chan"), split_axis=0, concat_axis=0, tiled=True
     )
     steps = make_steps(channel, recv.reshape(4 * CW, 128), *prepared)
     return lax.all_to_all(steps.reshape(BLOCKS, 1, 128), "stn", split_axis=0, concat_axis=0, tiled=True)

time: 64.3 us -> 64.4 us (level); the launches traced: 64.2 us -> 63.4 us
  blocking collectives: 55 us -> 54.2 us
where the time goes in v9:
time: 64.4 us; the launch traced here: 63.4 us
  blocking collectives  54.2 us (84%)
  Pallas kernels  8.63 us (13%)
    all_to_all x1, blocking collectives, body(): lax.all_to_all(payload.reshape(CW, 4, 128), ('stn', 'chan'), split_axis=0...  43.8 us
    all_to_all x1, blocking collectives, body(): lax.all_to_all(steps.reshape(BLOCKS, 1, 128), 'stn', split_axis=0, concat...  10.4 us
    pallas_call x1, Pallas kernels, make_spectra(): pl.pallas_call(spectra_kernel, out_shape=(pltpu.VMEM((4 * CW, 128), BF),...  5.06 us
    pallas_call x1, Pallas kernels, make_steps(): pl.pallas_call(pair_kernel, out_shape=jax.ShapeDtypeStruct((BLOCKS, 128),...  3.57 us

profile of v9, /device:TPU:1, one launch (start us, length us, event | category | flops | bytes accessed | tf_op | source)
XLA Modules:
  0.0 63.4 jit_solution(13233387714069802417)
XLA Ops:
  0.0 5.1 %spectra.1 = (bf16[2048,128]{1,0:T(8,128)(2,1)S(1)}, bf16[2,2,128,512]{3,2,1,0:T(8,128)(2,1)S(1)}, f32[512,128]{1,0:T(8,128)S(1)}, f32[512,128]{1,0:T(8,128)S(1)...) custom-call(s32[1]{0:T(128)} %bitcast.index_ref, ...), custom_call_target="tpu_custom_call" | custom-call | tf_op jit(solution)/shard_map/spectra/pallas_call | solution.py:421
  5.1 43.8 %all_to_all.10 = bf16[512,4,128]{2,1,0:T(4,128)(2,1)S(1)} all-to-all(bf16[512,4,128]{2,1,0:T(4,128)(2,1)S(1)} %bitcast.16), channel_id=1, replica_groups=mesh['chan'=32,'stn'=16] {'stn','chan'}, dimensions={0} | all-to-all | bytes 1048576 | tf_op jit(solution)/shard_map/all_to_all | solution.py:495
  48.8 3.6 %pairs.1 = f32[16,128]{1,0:T(8,128)S(1)} custom-call(s32[1]{0:T(128)} %bitcast.index_ref, bf16[2048,128]{1,0:T(8,128)(2,1)S(1)} %bitcast.15, bf16[2,2,128,512]{3,2,1,0:T(8,128)(2,1)S(1)} %get-tuple-element.15.near_e, f32[512,128]{1,0:T(8,128)S(1)} %get-tuple-element.16.steer_ref, f32[512,128]{1,0:T(8,128)S(1)} %get-tuple-element.17.turned_ref, ...), custom_call_target="tpu_custom_call" | custom-call | tf_op jit(solution)/shard_map/pairs/pallas_call | solution.py:470
  52.4 10.4 %all_to_all.11 = f32[16,1,128]{2,1,0:T(1,128)S(1)} all-to-all(f32[16,1,128]{2,1,0:T(1,128)S(1)} %bitcast.17), channel_id=1, replica_groups=mesh['chan'=32,'stn'=16] {'stn'}, dimensions={0} | all-to-all | bytes 16384 | tf_op jit(solution)/shard_map/all_to_all | solution.py:499
  62.8 0.6 copy.16
